TPU v7x, 256 devices: a whole 4x4x8 slice. The times are simulated.
256 devices in a mesh: dp: 8 (over z), seq: 32 (over y, x, core).
Axes of the slice: x: 4, y: 4, z: 8, core: 2. Of those that a mesh axis runs over, the one named last changes fastest.
Arguments:
- query_rows: bfloat16 [8, 4096, 512], P('dp', 'seq'), may hold values from -6 to 6
- key_rows: bfloat16 [8, 4096, 512], P('dp', 'seq'), may hold values from -6 to 6
- value_rows: bfloat16 [8, 4096, 512], P('dp', 'seq'), may hold values from -6 to 6
- inputs: bfloat16 [8, 4096, 1024], P('dp', 'seq'), may hold values from -6 to 6
- lengths: int32 [8], P('dp'), may hold values from 1024 to 4096, as said below
- out_weight: bfloat16 [512, 1024], replicated, may hold values from -0.25 to 0.25
- kernel: float32 [31, 1024], replicated, may hold values from -1 to 1
- norm_gain: float32 [1024], replicated, may hold values from 0.5 to 1.5
- norm_shift: float32 [1024], replicated, may hold values from -1 to 1
- cotangent: bfloat16 [8, 4096, 1024], P('dp', 'seq'), may hold values from -6 to 6
Outputs:
- output: bfloat16 [8, 4096, 1024], P('dp', 'seq')
- grad_inputs: bfloat16 [8, 4096, 1024], P('dp', 'seq')
- grad_query: bfloat16 [8, 4096, 512], P('dp', 'seq')
- grad_key: bfloat16 [8, 4096, 512], P('dp', 'seq')
- grad_value: bfloat16 [8, 4096, 512], P('dp', 'seq')
- grad_out_weight: float32 [512, 1024], replicated
- grad_kernel: float32 [31, 1024], replicated
- grad_gain: float32 [1024], replicated
- grad_shift: float32 [1024], replicated
Inputs may be any that keep to these rules, and one draw needn't show every extreme that they name: `lengths`: the longest recording has exactly 4096 valid frames.
All inputs are finite; a program needn't handle non-finite values.
Results may differ from a plain program's by a relative error of at most 0.028.
Values may be sent and summed in bfloat16 or wider, within the bound.
A program may use at most 128 MiB of HBM per device.

v0:
```python
import math

import jax
import jax.numpy as jnp
from jax import lax
from jax.sharding import PartitionSpec as P

HEADS = 8
KERNEL = 31


NEGATIVE = -1e30
EPSILON = 1e-05


def padded_2(array, sides, width):
    for axis, dim in sides:
        count, length = (lax.axis_size(axis), array.shape[dim])
        up = [(i, (i + 1) % count) for i in range(count - 1)]
        down = [(j, i) for i, j in up]
        last = lax.slice_in_dim(array, length - width, length, axis=dim)
        first = lax.slice_in_dim(array, 0, width, axis=dim)
        before = lax.ppermute(last, axis, up)
        after = lax.ppermute(first, axis, down)
        array = jnp.concatenate([before, array, after], axis=dim)
    return array


def split_heads(matrix):
    return matrix.reshape(matrix.shape[0], HEADS, matrix.shape[1] // HEADS)


def head_scores(queries, key_block):
    score_scale = (queries.shape[1] // HEADS) ** (-0.5)
    return (
        jnp.einsum(
            "qhd,khd->hqk",
            split_heads(queries),
            split_heads(key_block),
            preferred_element_type=jnp.float32,
        )
        * score_scale
    )


def over_blocks(compute, initial, block_rows, block_count):

    def over_advance(carried, block_index):
        block_start = block_index * block_rows
        return (compute(block_start, carried), None)

    finished, unused = lax.scan(over_advance, initial, jnp.arange(block_count, dtype=jnp.int32))
    return finished


def softmax_totals(queries, all_keys, key_live, block_rows):
    row_count = queries.shape[0]

    def compute(block_start, carried):
        highest, running_sum = carried
        key_block = lax.dynamic_slice_in_dim(all_keys, block_start, block_rows, 0)
        live_block = lax.dynamic_slice_in_dim(key_live, block_start, block_rows, 0)
        scores = jnp.where(live_block[None, None, :], head_scores(queries, key_block), NEGATIVE)
        new_high = jnp.maximum(highest, jnp.max(scores, axis=-1))
        running_sum = running_sum * jnp.exp(highest - new_high) + jnp.sum(
            jnp.exp(scores - new_high[:, :, None]), axis=-1
        )
        return (new_high, running_sum)

    initial = (
        jnp.full((HEADS, row_count), NEGATIVE, jnp.float32),
        jnp.zeros((HEADS, row_count), jnp.float32),
    )
    highest, running_sum = over_blocks(
        compute, initial, block_rows, all_keys.shape[0] // block_rows
    )
    return highest + jnp.log(running_sum)


def attend(queries, all_keys, all_values, key_live, log_total, block_rows):
    row_count, channels = queries.shape

    def compute(block_start, running):
        key_block = lax.dynamic_slice_in_dim(all_keys, block_start, block_rows, 0)
        value_block = lax.dynamic_slice_in_dim(all_values, block_start, block_rows, 0)
        live_block = lax.dynamic_slice_in_dim(key_live, block_start, block_rows, 0)
        weights = jnp.where(
            live_block[None, None, :],
            jnp.exp(head_scores(queries, key_block) - log_total[:, :, None]),
            0.0,
        ).astype(jnp.bfloat16)
        return running + jnp.einsum(
            "hqk,khd->qhd", weights, split_heads(value_block), preferred_element_type=jnp.float32
        )

    initial = jnp.zeros((row_count, HEADS, channels // HEADS), jnp.float32)
    summed = over_blocks(compute, initial, block_rows, all_keys.shape[0] // block_rows)
    return summed.reshape(row_count, channels).astype(jnp.bfloat16)


def joined_grads(
    queries, grad_context, log_total, row_delta, all_keys, all_values, key_live, block_rows
):
    row_count, channels = queries.shape
    score_scale = (channels // HEADS) ** (-0.5)
    total_rows = all_keys.shape[0]

    def joined_advance(running, block_index):
        block_start = block_index * block_rows
        key_block = lax.dynamic_slice_in_dim(all_keys, block_start, block_rows, 0)
        value_block = lax.dynamic_slice_in_dim(all_values, block_start, block_rows, 0)
        live_block = lax.dynamic_slice_in_dim(key_live, block_start, block_rows, 0)

        def compute(carried):
            weights = jnp.where(
                live_block[None, None, :],
                jnp.exp(head_scores(queries, key_block) - log_total[:, :, None]),
                0.0,
            )
            grad_value = jnp.einsum(
                "hqk,qhd->khd",
                weights.astype(jnp.bfloat16),
                split_heads(grad_context),
                preferred_element_type=jnp.float32,
            )
            grad_weights = jnp.einsum(
                "qhd,khd->hqk",
                split_heads(grad_context),
                split_heads(value_block),
                preferred_element_type=jnp.float32,
            )
            grad_scores = (weights * (grad_weights - row_delta[:, :, None])).astype(jnp.bfloat16)
            grad_key = (
                jnp.einsum(
                    "hqk,qhd->khd",
                    grad_scores,
                    split_heads(queries),
                    preferred_element_type=jnp.float32,
                )
                * score_scale
            )
            updated = carried + jnp.einsum(
                "hqk,khd->qhd",
                grad_scores,
                split_heads(key_block),
                preferred_element_type=jnp.float32,
            )
            block_terms = jnp.concatenate(
                [grad_key.reshape(block_rows, channels), grad_value.reshape(block_rows, channels)],
                axis=1,
            )
            return (updated, block_terms)

        return compute(running)

    initial = jnp.zeros((row_count, HEADS, channels // HEADS), jnp.float32)
    summed, stacked = lax.scan(
        joined_advance, initial, jnp.arange(total_rows // block_rows, dtype=jnp.int32)
    )
    grad_query = (summed * score_scale).reshape(row_count, channels).astype(jnp.bfloat16)
    return (grad_query, stacked.reshape(total_rows, 2 * channels))


def depthwise(padded, kernel, frames):
    result = jnp.zeros((frames, kernel.shape[1]), jnp.float32)
    for offset in range(kernel.shape[0]):
        result = result + kernel[offset] * padded[offset : offset + frames].astype(jnp.float32)
    return result


def shards(
    query_rows,
    key_rows,
    value_rows,
    inputs,
    lengths,
    out_weight,
    kernel,
    norm_gain,
    norm_shift,
    cotangent,
):
    frames = query_rows.shape[1]
    total_rows = frames * lax.axis_size("seq")
    block_rows = math.gcd(total_rows, 512)
    length = lengths[0]
    positions = lax.axis_index("seq") * frames + jnp.arange(frames, dtype=jnp.int32)
    frame_live = positions < length
    frame_mask = frame_live.astype(jnp.float32)[:, None]
    own_queries = query_rows[0]
    own_keys = key_rows[0]
    own_values = value_rows[0]
    all_keys, all_values = (
        lax.all_gather(own_keys, "seq", axis=0, tiled=True),
        lax.all_gather(own_values, "seq", axis=0, tiled=True),
    )
    key_live = jnp.arange(total_rows, dtype=jnp.int32) < length
    log_total = softmax_totals(own_queries, all_keys, key_live, block_rows)
    context = attend(own_queries, all_keys, all_values, key_live, log_total, block_rows)
    projected = jnp.dot(context, out_weight, preferred_element_type=jnp.float32)
    hidden = (frame_mask * (inputs[0].astype(jnp.float32) + projected)).astype(jnp.bfloat16)
    half_width = KERNEL // 2
    padded = padded_2(hidden, (("seq", 0),), half_width)
    conv_out = depthwise(padded, kernel, frames)
    local_count = jnp.sum(frame_mask)
    masked_conv = frame_mask * conv_out
    count_all, sum_all = lax.psum((local_count, jnp.sum(masked_conv, axis=0)), ("dp", "seq"))
    moment_mean = sum_all / count_all
    centered = conv_out - moment_mean
    variance = (
        lax.psum(jnp.sum(frame_mask * centered * centered, axis=0), ("dp", "seq")) / count_all
    )
    inverse = lax.rsqrt(variance + EPSILON)
    normed = centered * inverse
    act_in = normed * norm_gain + norm_shift
    gate_part = jax.nn.sigmoid(act_in)
    output = (frame_mask * (hidden.astype(jnp.float32) + act_in * gate_part)).astype(jnp.bfloat16)
    grad_out = frame_mask * cotangent[0].astype(jnp.float32)
    grad_act = grad_out * gate_part * (1.0 + act_in * (1.0 - gate_part))
    grad_gain, grad_shift = lax.psum(
        (jnp.sum(grad_act * normed, axis=0), jnp.sum(grad_act, axis=0)), ("dp", "seq")
    )
    grad_conv = (
        frame_mask
        * inverse
        * norm_gain
        * (grad_act - (grad_shift + normed * grad_gain) / count_all)
    )
    grad_padded = padded_2(grad_conv, (("seq", 0),), half_width)
    kernel_terms = jnp.stack(
        [
            jnp.sum(grad_conv * padded[offset : offset + frames].astype(jnp.float32), axis=0)
            for offset in range(KERNEL)
        ]
    )
    grad_hidden = grad_out
    for offset in range(KERNEL):
        grad_hidden = (
            grad_hidden
            + kernel[offset]
            * grad_padded[2 * half_width - offset : 2 * half_width - offset + frames]
        )
    grad_inputs = (frame_mask * grad_hidden).astype(jnp.bfloat16)
    weight_terms = jnp.einsum("ta,td->ad", context, grad_inputs, preferred_element_type=jnp.float32)
    grad_kernel, grad_out_weight = lax.psum((kernel_terms, weight_terms), ("dp", "seq"))
    grad_context = jnp.einsum(
        "td,ad->ta", grad_inputs, out_weight, preferred_element_type=jnp.float32
    ).astype(jnp.bfloat16)
    row_delta = jnp.transpose(
        jnp.sum(
            split_heads(context.astype(jnp.float32) * grad_context.astype(jnp.float32)), axis=-1
        )
    )
    channels = own_queries.shape[1]
    grad_query, key_terms_all = joined_grads(
        own_queries, grad_context, log_total, row_delta, all_keys, all_values, key_live, block_rows
    )
    summed = lax.psum_scatter(
        key_terms_all.astype(jnp.bfloat16), "seq", scatter_dimension=0, tiled=True
    ).astype(jnp.float32)
    grad_key = summed[:, :channels].astype(jnp.bfloat16)
    grad_value = summed[:, channels:].astype(jnp.bfloat16)
    return (
        output[None],
        grad_inputs[None],
        grad_query[None],
        grad_key[None],
        grad_value[None],
        grad_out_weight,
        grad_kernel,
        grad_gain,
        grad_shift,
    )


def solution(mesh):
    in_specs = (
        P("dp", "seq", None),
        P("dp", "seq", None),
        P("dp", "seq", None),
        P("dp", "seq", None),
        P("dp"),
        P(),
        P(),
        P(),
        P(),
        P("dp", "seq", None),
    )
    out_specs = (
        P("dp", "seq", None),
        P("dp", "seq", None),
        P("dp", "seq", None),
        P("dp", "seq", None),
        P("dp", "seq", None),
        P(),
        P(),
        P(),
        P(),
    )
    return jax.shard_map(shards, mesh=mesh, in_specs=in_specs, out_specs=out_specs, check_vma=False)
```

profile of v0, /device:TPU:1, one launch (start us, length us, event | category | flops | bytes accessed | tf_op | source)
XLA Modules:
  0.0 894.5 jit_solution(5822555584343116064)
XLA Ops:
  7.2 1.7 copy.29
  9.1 1.7 copy.28
  13.1 2.0 fusion.209
  16.2 53.4 %all-gather.7.cloned.1.call-done = bf16[1,4096,512]{1,2,0:T(8,128)(2,1)} async-done(((bf16[1,128,512]{1,2,0:T(8,128)(2,1)}), bf16[1,4096,512]{1,2,0:T(8,128)(2,1)}) %all-gather.7.cloned.1.call-update) | async-done | bytes 4194320 | tf_op jit(solution)/shard_map/all_gather | solution.py:194
  69.6 35.3 %while.37 = (s32[]{:T(128)}, f32[8,128]{1,0:T(8,128)S(1)}, f32[8,128]{1,0:T(8,128)S(1)}, s32[8]{0:T(128)S(1)}, pred[4096]{0:T(1024)(128)(4,1)}, /*index=5*/bf16[...) while((s32[]{:T(128)}, f32[8,128]{1,0:T(8,128)S(1)}, ...), condition=%wide.region_3.4_spmd.clone, body=%wide.region_0.3_spmd.clone.sunk | while | flops 70784008 | bytes 5954042 | solution.py:52
  105.5 21.0 %all-gather.5.cloned.1.call-done = bf16[1,4096,512]{1,2,0:T(8,128)(2,1)} async-done(((bf16[1,128,512]{1,2,0:T(8,128)(2,1)}), bf16[1,4096,512]{1,2,0:T(8,128)(2,1)}) %all-gather.5.cloned.1.call-update) | async-done | bytes 4194320 | tf_op jit(solution)/shard_map/all_gather | solution.py:195
  126.5 38.7 %while.38 = (s32[]{:T(128)}, f32[128,8,64]{0,2,1:T(8,128)S(1)}, s32[8]{0:T(128)S(1)}, bf16[4096,512]{0,1:T(8,128)(2,1)}, pred[4096]{0:T(1024)(128)(4,1)}, /*inde...) while((s32[]{:T(128)}, f32[128,8,64]{0,2,1:T(8,128)S(1)}, ...), condition=%wide.region_5.6_spmd.clone, body=%wide.region_4.5_spmd.clone.sunk | while | flops 136445952 | bytes 3806921 | solution.py:52
  127.8 1.3 constant_dynamic-slice_fusion.9
  129.8 1.5 fusion.260
  134.6 1.5 fusion.260
  137.4 1.3 constant_dynamic-slice_fusion.9
  139.5 1.5 fusion.260
  142.3 1.3 constant_dynamic-slice_fusion.9
  144.3 1.5 fusion.260
  149.2 1.5 fusion.260
  152.0 1.3 constant_dynamic-slice_fusion.9
  154.0 1.5 fusion.260
  156.8 1.3 constant_dynamic-slice_fusion.9
  158.9 1.5 fusion.260
  163.7 1.5 fusion.260
  165.9 2.2 collective-permute-start.1
  168.1 3.4 collective-permute-start
  172.9 2.6 multiply_reduce_fusion.1
  175.4 78.9 %all-reduce.1 = (f32[1024]{0:T(1024)S(1)}, f32[]{:T(128)}) all-reduce(f32[1024]{0:T(1024)S(1)} %get-tuple-element.394, f32[]{:T(128)} %get-tuple-element.392), channel_id=1, replica_groups=mesh['dp'=8,'seq'=32] {'dp','seq'}, use_global_device_ids=true, to_apply=%region_7.8 | all-reduce | flops 1025 | bytes 8200 | tf_op jit(solution)/shard_map/psum | solution.py:207
  255.2 73.3 %psum.51 = f32[1024]{0:T(1024)S(1)} all-reduce(f32[1024]{0:T(1024)S(1)} %fusion.170), channel_id=1, replica_groups=mesh['dp'=8,'seq'=32] {'dp','seq'}, use_global_device_ids=true, to_apply=%region_11.12 | all-reduce | flops 1024 | bytes 8192 | tf_op jit(solution)/shard_map/psum | solution.py:211
  330.3 73.2 %all-reduce = (f32[1024]{0:T(1024)S(1)}, f32[1024]{0:T(1024)S(1)}) all-reduce(f32[1024]{0:T(1024)S(1)} %get-tuple-element.331, f32[1024]{0:T(1024)S(1)} %get-tuple-element.330), channel_id=1, replica_groups=mesh['dp'=8,'seq'=32] {'dp','seq'}, use_global_device_ids=true, to_apply=%region_15.16 | all-reduce | flops 2048 | bytes 16384 | tf_op jit(solution)/shard_map/psum | solution.py:220
  403.5 3.5 fusion.166
  407.0 3.3 collective-permute-start.3
  410.3 2.1 collective-permute-start.2
  412.5 3.3 collective-permute-done.2
  415.9 2.5 fusion.23
  419.3 85.6 %while.39 = (s32[]{:T(128)}, f32[128,8,64]{0,2,1:T(8,128)}, bf16[8,512,1024]{1,2,0:T(8,128)(2,1)}, s32[8]{0:T(128)S(1)}, bf16[4096,512]{0,1:T(8,128)(2,1)}, /*in...) while((s32[]{:T(128)}, f32[128,8,64]{0,2,1:T(8,128)}, ...), condition=%wide.region_18.19_spmd.clone, body=%wide.region_17.18_spmd.clone.sunk | while | flops 341966848 | bytes 34088732 | solution.py:157
  420.6 1.3 constant_dynamic-slice_fusion.10
  422.6 1.4 exponential_select_fusion.2
  424.1 1.3 copy-done.1
  431.0 1.3 constant_dynamic-slice_fusion.10
  433.0 1.4 exponential_select_fusion.2
  434.4 1.3 copy-done.1
  436.3 2.1 fusion.271
  443.7 1.4 exponential_select_fusion.2
  445.2 1.3 copy-done.1
  447.0 2.1 fusion.271
  454.5 1.4 exponential_select_fusion.2
  455.9 1.3 copy-done.1
  457.8 2.1 fusion.271
  465.2 1.4 exponential_select_fusion.2
  466.6 1.3 copy-done.1
  468.5 2.1 fusion.271
  476.0 1.4 exponential_select_fusion.2
  477.4 1.3 copy-done.1
  479.3 2.1 fusion.271
  486.7 1.4 exponential_select_fusion.2
  488.1 1.3 copy-done.1
  490.0 2.1 fusion.271
  497.4 1.4 exponential_select_fusion.2
  498.9 1.3 copy-done.1
  500.7 2.1 fusion.271
  504.9 11.5 %copy.36 = bf16[8,512,1024]{2,1,0:T(8,128)(2,1)} copy(bf16[8,512,1024]{1,2,0:T(8,128)(2,1)} %get-tuple-element.151) | data formatting | bytes 16777216 | tf_op jit(solution)/shard_map/convert_element_type | solution.py:259
  519.1 2.6 stack.127
  521.7 1.7 fusion.211
  524.3 91.5 %reduce-scatter.2.cloned.1.call-done = bf16[128,1024]{1,0:T(8,128)(2,1)} async-done(((bf16[4096,1024]{1,0:T(8,128)(2,1)}), bf16[128,1024]{1,0:T(8,128)(2,1)}) %reduce-scatter.2.cloned.1.call-update) | async-done | bytes 262160 | tf_op jit(solution)/shard_map/reduce_scatter | solution.py:258
  615.8 1.7 slice_bitcast_fusion
  617.4 266.7 %all-reduce.5.cloned.1.call-done = (f32[512,1024]{1,0:T(8,128)}, f32[31,1024]{1,0:T(8,128)}) async-done(((f32[512,1024]{1,0:T(8,128)}, f32[31,1024]{1,0:T(8,128)}), (f32[512,1024]{1,0:T(8,128)}, f32[31,1024]{1,0:T(8,128)})) %all-reduce.5.cloned.1.call-update) | async-done | bytes 2224144 | tf_op jit(solution)/shard_map/psum | solution.py:245
  884.1 3.2 copy.66
  (325 shorter events, 97.8 us)
Async XLA Ops:
  7.2 158.3 %copy-start = (bf16[512,1024]{1,0:T(8,128)(2,1)S(1)}, bf16[512,1024]{1,0:T(8,128)(2,1)}, u32[]{:S(2)}) copy-start(bf16[512,1024]{1,0:T(8,128)(2,1)} %param.21) | copy-start | bytes 3145732
  7.2 62.4 %all-gather.7.cloned.1.call-start = ((), (), s32[]{:S(2)}) async-start(), calls=%async_computation.3 | async-start | bytes 4325376 | tf_op jit(solution)/shard_map/all_gather | solution.py:194
  9.0 117.5 %all-gather.5.cloned.1.call-start = ((), (), s32[]{:S(2)}) async-start(), calls=%async_computation.2 | async-start | bytes 4325376 | tf_op jit(solution)/shard_map/all_gather | solution.py:195
  10.7 605.0 %reduce-scatter.2.cloned.1.call-start = ((), (), s32[]{:S(2)}) async-start(), calls=%async_computation.1 | async-start | bytes 8650752 | tf_op jit(solution)/shard_map/reduce_scatter | solution.py:258
  69.6 3.1 copy-start.46
  74.0 3.1 copy-start.46
  78.4 3.1 copy-start.46
  82.8 3.1 copy-start.46
  87.3 3.1 copy-start.46
  91.7 3.1 copy-start.46
  96.1 3.1 copy-start.46
  100.5 3.1 copy-start.46
  126.5 39.0 %copy-start.15 = (bf16[1,128,1024]{2,1,0:T(8,128)(2,1)S(1)}, bf16[1,128,1024]{2,1,0:T(8,128)(2,1)}, u32[]{:S(2)}) copy-start(bf16[1,128,1024]{2,1,0:T(8,128)(2,1)} %param.19) | copy-start | bytes 786436
  126.5 39.0 %copy-start.36 = (f32[128]{0:T(128)S(1)}, f32[128]{0:T(128)}, u32[]{:S(2)}) copy-start(f32[128]{0:T(128)} %get-tuple-element.393) | copy-start | bytes 1540
  165.2 7.4 copy-start.17
  165.3 7.4 copy-start.18
  165.3 7.4 copy-start.19
  165.3 7.4 copy-start.20
  165.3 7.4 copy-start.21
  165.3 7.4 copy-start.22
  165.3 7.4 copy-start.23
  165.3 7.4 copy-start.24
  165.3 7.4 copy-start.25
  165.3 7.4 copy-start.26
  165.4 7.4 copy-start.27
  165.4 7.4 copy-start.28
  165.4 7.4 copy-start.29
  165.4 7.4 copy-start.30
  165.4 7.4 copy-start.31
  165.4 7.4 copy-start.32
  165.4 7.4 copy-start.33
  165.4 7.4 copy-start.34
  165.4 7.4 copy-start.35
  165.4 163.7 %copy-start.8 = (bf16[1,128,1024]{2,1,0:T(8,128)(2,1)S(1)}, bf16[1,128,1024]{2,1,0:T(8,128)(2,1)}, u32[]{:S(2)}) copy-start(bf16[1,128,1024]{2,1,0:T(8,128)(2,1)} %param.25) | copy-start | bytes 786436
  165.5 163.7 %copy-start.37 = (f32[1024]{0:T(1024)S(1)}, f32[1024]{0:T(1024)}, u32[]{:S(2)}) copy-start(f32[1024]{0:T(1024)} %param.24) | copy-start | bytes 12292
  165.5 163.7 %copy-start.38 = (f32[1024]{0:T(1024)S(1)}, f32[1024]{0:T(1024)}, u32[]{:S(2)}) copy-start(f32[1024]{0:T(1024)} %param.23) | copy-start | bytes 12292
  165.5 246.9 %copy-start.9 = (bf16[128,8,64]{0,2,1:T(8,128)(2,1)}, bf16[128,8,64]{0,2,1:T(8,128)(2,1)S(1)}, u32[]{:S(2)}) copy-start(bf16[128,8,64]{0,2,1:T(8,128)(2,1)S(1)} %convert_element_type.201) | copy-start | bytes 393220
  165.9 241.1 %copy-start.3 = (bf16[128,1024]{1,0:T(8,128)(2,1)}, bf16[128,1024]{1,0:T(8,128)(2,1)S(1)}, u32[]{:S(2)}) copy-start(bf16[128,1024]{1,0:T(8,128)(2,1)S(1)} %fusion.17) | copy-start | bytes 786436
  165.9 6.7 collective-permute-start.1
  168.1 4.6 collective-permute-start
  172.7 234.3 %copy-start.11 = (bf16[15,1024]{1,0:T(8,128)(2,1)}, bf16[15,1024]{1,0:T(8,128)(2,1)S(1)}, u32[]{:S(2)}) copy-start(bf16[15,1024]{1,0:T(8,128)(2,1)S(1)} %collective-permute-done.1) | copy-start | bytes 92164
  172.7 230.8 %copy-start.13 = (bf16[15,1024]{1,0:T(8,128)(2,1)}, bf16[15,1024]{1,0:T(8,128)(2,1)S(1)}, u32[]{:S(2)}) copy-start(bf16[15,1024]{1,0:T(8,128)(2,1)S(1)} %collective-permute-done) | copy-start | bytes 92164
  403.5 15.3 %copy-start.44 = (f32[1024]{0:T(1024)}, f32[1024]{0:T(1024)S(1)}, u32[]{:S(2)}) copy-start(f32[1024]{0:T(1024)S(1)} %get-tuple-element.734) | copy-start | bytes 12292
  403.5 15.4 %copy-start.45 = (f32[1024]{0:T(1024)}, f32[1024]{0:T(1024)S(1)}, u32[]{:S(2)}) copy-start(f32[1024]{0:T(1024)S(1)} %get-tuple-element.735) | copy-start | bytes 12292
  407.0 5.5 collective-permute-start.3
  410.3 5.6 collective-permute-start.2
  425.9 1.7 copy-start.2
  436.3 2.1 copy-start.2
  447.0 2.1 copy-start.2
  457.8 2.1 copy-start.2
  468.5 2.1 copy-start.2
  479.3 2.1 copy-start.2
  490.0 2.1 copy-start.2
  500.7 2.1 copy-start.2
  516.4 2.6 copy-start.39
  516.4 2.6 copy-start.40
  516.4 2.6 copy-start.41
  516.4 2.6 copy-start.42
  516.5 2.6 copy-start.43
  516.5 5.2 copy-start.7
  516.5 5.2 copy-start.10
  516.5 367.6 %all-reduce.5.cloned.1.call-start = ((), (), s32[]{:S(2)}) async-start(), calls=%async_computation.4 | async-start | bytes 4456448 | tf_op jit(solution)/shard_map/psum | solution.py:245
  521.7 1.8 copy-start.5
  884.1 3.2 copy-start.16
  (20 other events, 19.9 us)
Sparse Core Ops, SparseCore 0:
  11.1 58.4 all-gather.6
  72.6 53.8 all-gather.4
  516.5 99.1 reduce-scatter.1
  622.6 261.4 all-reduce.4
where the time goes:
time: 899 us; the launch traced here: 895 us
  waiting for transfers between devices  436 us (48%)
  blocking collectives  225 us (25%)
  local copies, waits for them, and re-layouts  103 us (11%)
  matrix products  59.2 us (7%)
  other arithmetic  27.8 us (3%)
  loops' own time  16.8 us (2%)
  between operations  15.3 us (2%)
  starting transfers between devices  11.1 us (1%)
    psum x1, waiting for transfers between devices, shards(): lax.psum((kernel_terms, weight_terms), ('dp', 'seq'))  267 us
    reduce_scatter x1, waiting for transfers between devices, shards(): lax.psum_scatter(key_terms_all.astype(jnp.bfloat16), 'seq', scatter_dimen...  91.5 us
    psum x1, blocking collectives, shards(): lax.psum((local_count, jnp.sum(masked_conv, axis=0)), ('dp', 'seq'))  78.9 us
    psum x1, blocking collectives, shards(): lax.psum(jnp.sum(frame_mask * centered * centered, axis=0), ('dp', 'seq'))  73.3 us
    psum x1, blocking collectives, shards(): lax.psum((jnp.sum(grad_act * normed, axis=0), jnp.sum(grad_act, axis=0)),...  73.2 us
    all_gather x1, waiting for transfers between devices, shards(): lax.all_gather(own_keys, 'seq', axis=0, tiled=True)  53.4 us
    all_gather x1, waiting for transfers between devices, shards(): lax.all_gather(own_values, 'seq', axis=0, tiled=True)  21 us
    dynamic_slice x16, local copies, waits for them, and re-layouts, compute(): key_block = lax.dynamic_slice_in_dim(all_keys, block_start, block_rows, 0)  18.8 us
  transfers between devices with their start and end apart: 8, of which 5 were waited for; matrix products, arithmetic and copies ran while one was open for 5% of the time, Pallas kernels for 0%

commit v1 on v0

v1 whole, which is shorter than its diff:
```python
import functools

import jax
import jax.numpy as jnp
from jax import lax
from jax.experimental import pallas as pl
from jax.experimental.pallas import tpu as pltpu
from jax.sharding import PartitionSpec as P

KERNEL = 31
HALF = 15
HEAD_DIM = 64
ROWS = 128
HALO = 32
NEGATIVE = -1e30
EPSILON = 1e-05
KEY_BLOCK = 512
QUERY_BLOCK = 256
MESH = pl.DeviceIdType.MESH
F32 = jnp.float32
BF16 = jnp.bfloat16


def roll64(x):
    return pltpu.roll(x, 64, 1)


def low_lanes(shape):
    return lax.broadcasted_iota(jnp.int32, shape, 1) < 64


def split_units(x):
    rows = x.shape[0]
    units = x.reshape(rows // 32, 2, 16, 128)
    return units[:, 0].reshape(rows // 2, 128), units[:, 1].reshape(rows // 2, 128)


def join_units(first, second):
    rows = first.shape[0]
    first = first.reshape(rows // 16, 1, 16, 128)
    second = second.reshape(rows // 16, 1, 16, 128)
    return jnp.concatenate([first, second], axis=1).reshape(2 * rows, 128)


def pack_pair(x):
    first, second = split_units(x)
    low = low_lanes(first.shape)
    even = jnp.where(low, first, roll64(second))
    odd = jnp.where(low, roll64(first), second)
    return even, odd


def unpack_pair(even, odd):
    low = low_lanes(even.shape)
    return join_units(jnp.where(low, even, roll64(odd)), jnp.where(low, roll64(even), odd))


def unpack_low(packed):
    low = low_lanes(packed.shape)
    return join_units(jnp.where(low, packed, 0.0), jnp.where(low, roll64(packed), 0.0))


def unpack_high(packed):
    low = low_lanes(packed.shape)
    return join_units(jnp.where(low, 0.0, roll64(packed)), jnp.where(low, 0.0, packed))


def pack_low(x):
    first, second = split_units(x)
    return jnp.where(low_lanes(first.shape), first, roll64(second))


def pack_high(x):
    first, second = split_units(x)
    return jnp.where(low_lanes(first.shape), roll64(first), second)


def dot(a, b, dims=((1,), (0,))):
    return lax.dot_general(a, b, (dims, ((), ())), preferred_element_type=F32)


def shifted(x, amount):
    return x if amount == 0 else pltpu.roll(x, x.shape[0] - amount, 0)


def kernel(
    heads,
    seq,
    depth,
    length_ref,
    q_ref,
    k_ref,
    v_ref,
    x_hbm,
    cot_hbm,
    w_hbm,
    taps_hbm,
    gain_ref,
    shift_ref,
    out_ref,
    ginp_ref,
    gq_ref,
    gk_ref,
    gv_ref,
    gfin_ref,
    sums_ref,
    kv_send,
    q_send,
    kvbuf,
    qpk,
    k1,
    v1,
    kt,
    v1t,
    qaug,
    qcl,
    sbuf,
    pt,
    ctxh,
    linv,
    ctx_send,
    ctx_recv,
    x_ext,
    cot_ext,
    w_ref,
    taps_ref,
    ctx_ref,
    hid_ref,
    conv_ref,
    ga_ref,
    stat_a,
    stat_b,
    recv_a,
    recv_b,
    stat_c,
    recv_c,
    stat_d,
    recv_d,
    tot_ref,
    do_send,
    do_recv,
    doaug,
    docl,
    rbuf,
    dqt,
    dsend,
    precv,
    osend,
    kvrecv,
    dq_send,
    dq_recv,
    wsend,
    g0,
    gs1,
    g1,
    gs2,
    g2,
    load_sem,
    send,
    recv,
    ctx_sem,
    dq_sem,
    part_send,
    part_recv,
    own_sem,
):
    chips = seq // 2
    width = q_ref.shape[1]
    channels = out_ref.shape[1]
    chunks = channels // 128
    queries = ROWS * heads
    half_keys = chips * ROWS
    half_blocks = half_keys // KEY_BLOCK
    query_blocks = queries // QUERY_BLOCK
    padded = channels + 128
    ext = ROWS + 2 * HALO
    mid = ROWS + 32

    z = lax.axis_index("dp")
    me = lax.axis_index("seq")
    chip = me // 2
    core = me % 2
    other = 1 - core
    partner = (z, chip * 2 + other)
    group = (chip // heads) * 2 + core
    my_group = me // heads
    length = length_ref[0]

    def remote(src, dst, send_sem, recv_sem, device):
        return pltpu.make_async_remote_copy(
            src_ref=src, dst_ref=dst, send_sem=send_sem, recv_sem=recv_sem, device_id=device, device_id_type=MESH
        )

    def drain(ref, sem):
        pltpu.make_async_copy(ref, ref, sem).wait()

    barrier = pltpu.get_barrier_semaphore()

    @pl.loop(1, seq)
    def _(d):
        pl.semaphore_signal(barrier, inc=1, device_id=(z, (me + d) % seq), device_id_type=MESH)

    @pl.loop(1, depth)
    def _(d):
        for c in range(2):
            pl.semaphore_signal(
                barrier, inc=1, device_id=((z + d) % depth, chip * 2 + c), device_id_type=MESH
            )

    own_x = pltpu.make_async_copy(x_hbm, x_ext.at[pl.ds(HALO, ROWS)], load_sem.at[0])
    own_cot = pltpu.make_async_copy(cot_hbm, cot_ext.at[pl.ds(16, ROWS)], load_sem.at[1])
    load_w = pltpu.make_async_copy(w_hbm, w_ref, load_sem.at[2])
    load_taps = pltpu.make_async_copy(taps_hbm, taps_ref, load_sem.at[3])
    own_x.start()
    own_cot.start()
    load_w.start()
    load_taps.start()

    for pair in range(heads // 2):
        columns = slice(128 * pair, 128 * pair + 128)
        kp = k_ref[:, columns].astype(F32)
        vp = v_ref[:, columns].astype(F32)
        low = low_lanes(kp.shape)
        kv_send[2 * pair] = jnp.where(low, kp, roll64(vp)).astype(BF16)
        kv_send[2 * pair + 1] = jnp.where(low, roll64(kp), vp).astype(BF16)
        even, odd = pack_pair(q_ref[:, columns].astype(F32))
        q_send[2 * pair] = even.astype(BF16)
        q_send[2 * pair + 1] = odd.astype(BF16)

    pl.semaphore_wait(barrier, seq - 1 + 2 * (depth - 1))

    kv_slot = pl.ds(core * half_keys + chip * ROWS, ROWS)
    pltpu.make_async_copy(kv_send.at[chip % heads], kvbuf.at[kv_slot], recv.at[0]).start()

    @pl.loop(1, chips)
    def _(d):
        peer = (chip + d) % chips
        remote(
            kv_send.at[peer % heads], kvbuf.at[kv_slot], send.at[0], recv.at[0], (z, peer * 2 + core)
        ).start()

    def head_device(head):
        return ((my_group // 2) * heads + head) * 2 + my_group % 2

    def to_heads(source, target, index, self_index):
        head = chip % heads
        slot = me % heads
        mine = head_device(head) == me

        @pl.when(mine)
        def _():
            pltpu.make_async_copy(source.at[head], target.at[slot], recv.at[index]).start()

        @pl.when(jnp.logical_not(mine))
        def _():
            remote(
                source.at[head], target.at[slot], send.at[self_index], recv.at[index], (z, head_device(head))
            ).start()

        @pl.loop(1, heads)
        def _(d):
            to = (chip + d) % heads
            remote(
                source.at[to], target.at[slot], send.at[index], recv.at[index], (z, head_device(to))
            ).start()

    def to_heads_done(target, index, self_index):
        drain(target.at[pl.ds(0, heads - 1)], send.at[index])

        @pl.when(head_device(chip % heads) != me)
        def _():
            drain(target.at[0], send.at[self_index])

    to_heads(q_send, qpk, 1, 2)

    after = (z, (me + 1) % seq)
    before = (z, (me + seq - 1) % seq)
    own_x.wait()
    own_cot.wait()
    halo_copies = (
        remote(x_ext.at[pl.ds(ROWS, HALO)], x_ext.at[pl.ds(0, HALO)], send.at[3], recv.at[3], after),
        remote(x_ext.at[pl.ds(HALO, HALO)], x_ext.at[pl.ds(HALO + ROWS, HALO)], send.at[4], recv.at[4], before),
        remote(cot_ext.at[pl.ds(ROWS, 16)], cot_ext.at[pl.ds(0, 16)], send.at[5], recv.at[5], after),
        remote(cot_ext.at[pl.ds(16, 16)], cot_ext.at[pl.ds(16 + ROWS, 16)], send.at[6], recv.at[6], before),
    )
    for copy in halo_copies:
        copy.start()

    mine_half = kvbuf.at[pl.ds(core * half_keys, half_keys)]
    drain(mine_half, recv.at[0])
    forward = remote(mine_half, mine_half, send.at[7], recv.at[7], partner)
    forward.start()

    def prepare_keys(half):
        @pl.loop(0, half_blocks)
        def _(block):
            start = pl.multiple_of(half * half_keys + block * KEY_BLOCK, KEY_BLOCK)
            rows = pl.ds(start, KEY_BLOCK)
            kv = kvbuf[rows].astype(F32)
            lane = lax.broadcasted_iota(jnp.int32, kv.shape, 1)
            row = lax.broadcasted_iota(jnp.int32, kv.shape, 0) + block * KEY_BLOCK
            frame = ((row >> 7) * 2 + half) * ROWS + (row & 127)
            bias = jnp.where(jnp.logical_and(lane == 64, frame >= length), NEGATIVE, 0.0)
            keyed = jnp.where(lane < 64, kv, bias)
            valued = jnp.where(lane < 64, 1.0, kv)
            k1[rows] = keyed.astype(BF16)
            v1[rows] = valued.astype(BF16)
            kt[:, rows] = jnp.transpose(kv)[:64].astype(BF16) * BF16(0.125)
            v1t[:, rows] = jnp.transpose(valued).astype(BF16)

    prepare_keys(core)

    drain(qpk, recv.at[1])
    for index in range(heads):
        rows = slice(ROWS * index, ROWS * index + ROWS)
        part = unpack_low(qpk[index].astype(F32))
        lane = lax.broadcasted_iota(jnp.int32, part.shape, 1)
        qcl[rows] = (part * 0.125).astype(BF16)
        qaug[rows] = jnp.where(lane == 64, 1.0, part).astype(BF16)

    forward.wait_recv()
    prepare_keys(other)

    key_blocks = 2 * half_blocks
    factor = 0.125 * 1.4426950408889634

    def scores_step(query_block, block, highest):
        rows = pl.ds(pl.multiple_of(block * KEY_BLOCK, KEY_BLOCK), KEY_BLOCK)
        scores = dot(
            k1[rows], qaug[query_block * QUERY_BLOCK : (query_block + 1) * QUERY_BLOCK], ((1,), (1,))
        )
        sbuf[query_block % 2, rows] = scores
        return jnp.maximum(highest, jnp.max(scores.reshape(KEY_BLOCK // 8, 8, QUERY_BLOCK), axis=0))

    def weights_step(query_block, block, highest, total):
        rows = pl.ds(pl.multiple_of(block * KEY_BLOCK, KEY_BLOCK), KEY_BLOCK)
        weights = jnp.exp2((sbuf[query_block % 2, rows] - highest) * factor).astype(BF16)
        pt[rows, query_block * QUERY_BLOCK : (query_block + 1) * QUERY_BLOCK] = weights
        return total + dot(v1t[:, rows], weights)

    def context_finish(query_block, total):
        turned = jnp.transpose(total)
        low = low_lanes(turned.shape)
        inverse = 1.0 / jnp.where(low, 1.0, roll64(turned))
        context = jnp.where(low, 0.0, turned * inverse).astype(BF16).astype(F32)
        rows = slice(query_block * QUERY_BLOCK, (query_block + 1) * QUERY_BLOCK)
        linv[rows] = inverse
        ctxh[rows] = context
        half_rows = slice(query_block * QUERY_BLOCK // 2, (query_block + 1) * QUERY_BLOCK // 2)
        ctx_send[half_rows] = pack_high(context).astype(BF16)

    start_high = jnp.full((8, QUERY_BLOCK), NEGATIVE, F32)
    start_total = jnp.zeros((128, QUERY_BLOCK), F32)
    high = lax.fori_loop(0, key_blocks, lambda b, h: scores_step(0, b, h), start_high)
    for block in range(query_blocks):
        highest = jnp.max(high, axis=0, keepdims=True)
        if block + 1 < query_blocks:

            def both(b, carried, block=block, highest=highest):
                h, t = carried
                return scores_step(block + 1, b, h), weights_step(block, b, highest, t)

            high, total = lax.fori_loop(0, key_blocks, both, (start_high, start_total))
        else:
            total = lax.fori_loop(
                0,
                key_blocks,
                lambda b, t, block=block, highest=highest: weights_step(block, b, highest, t),
                start_total,
            )
        context_finish(block, total)

    my_head = chip % heads
    moves = [(-1, 0, 16, 80), (0, 0, 80, 16)]
    moves += [(i, 64 * i - 16, 96, 0) for i in range(1, heads - 1)]
    moves += [(heads - 1, 64 * (heads - 1) - 16, 80, 0), (heads, 64 * heads - 16, 16, 0)]

    def owner_of(i):
        return (group * heads + i + seq) % seq

    for index, (i, start, count, to) in enumerate(moves):
        source = ctx_send.at[pl.ds(start, count)]
        target = ctx_recv.at[my_head, pl.ds(to, count)]

        @pl.when(owner_of(i) == me)
        def _(source=source, target=target):
            pltpu.make_async_copy(source, target, recv.at[8]).start()

        @pl.when(owner_of(i) != me)
        def _(source=source, target=target, i=i, index=index):
            remote(source, target, ctx_sem.at[index], recv.at[8], (z, owner_of(i))).start()

    load_w.wait()
    load_taps.wait()
    for copy in halo_copies:
        copy.wait_recv()
    drain(ctx_recv, recv.at[8])

    for pair in range(heads // 2):
        ctx_ref[:, 128 * pair : 128 * pair + 128] = unpack_pair(
            ctx_recv[2 * pair].astype(F32), ctx_recv[2 * pair + 1].astype(F32)
        ).astype(BF16)

    def live(rows, first):
        frame = me * ROWS + first + lax.broadcasted_iota(jnp.int32, (rows, 128), 0)
        return jnp.logical_and(frame >= 0, frame < length)

    def column(chunk):
        return pl.ds(pl.multiple_of(chunk * 128, 128), 128)

    counted = jnp.clip(length - me * ROWS, 0, ROWS).astype(F32)

    @pl.loop(0, channels // 256)
    def _(chunk):
        columns = pl.ds(pl.multiple_of(chunk * 256, 256), 256)
        hidden = x_ext[:, columns].astype(F32) + dot(ctx_ref[...], w_ref[:, columns])
        mask = live(ext, -HALO)
        mask = jnp.concatenate([mask, mask], axis=1)
        hid_ref[:, columns] = jnp.where(mask, hidden, 0.0).astype(BF16).astype(F32)

    @pl.loop(0, chunks)
    def _(chunk):
        columns = column(chunk)
        hidden = hid_ref[:, columns]
        total = jnp.zeros((mid, 128), F32)
        for low in range(8):
            moved = shifted(hidden, low)
            for high_part in range(4):
                tap = 8 * high_part + low - 1
                if 0 <= tap < KERNEL:
                    total = total + taps_ref[tap : tap + 1, columns] * moved[8 * high_part : 8 * high_part + mid]
        conv_ref[:, columns] = total
        own = total[16 : 16 + ROWS]
        mask = live(ROWS, 0)
        summed = jnp.sum(jnp.where(mask, own, 0.0), axis=0, keepdims=True)
        mean = summed / jnp.maximum(counted, 1.0)
        spread = own - mean
        squares = jnp.sum(jnp.where(mask, spread * spread, 0.0), axis=0, keepdims=True)
        stat_a[pl.ds(chunk, 1)] = summed
        stat_a[pl.ds(chunks + chunk, 1)] = squares

    stat_a[2 * chunks :] = jnp.full((chunks, 128), counted, F32)

    def gather_first(source, target, index):
        slot = z * 2 + core
        target[slot] = source[...]
        remote(source, target.at[slot], send.at[index], recv.at[index], partner).start()

        @pl.loop(1, depth)
        def _(d):
            for c in range(2):
                remote(
                    source, target.at[slot], send.at[index], recv.at[index], ((z + d) % depth, chip * 2 + c)
                ).start()

        drain(target.at[pl.ds(0, 2 * depth - 1)], recv.at[index])

    def gather_second(source, target, index):
        target[chip] = source[...]

        @pl.loop(1, chips)
        def _(d):
            remote(
                source, target.at[chip], send.at[index], recv.at[index], (z, ((chip + d) % chips) * 2 + core)
            ).start()

        drain(target.at[pl.ds(0, chips - 1)], recv.at[index])

    def merged(gathered):
        sums = gathered[:, :chunks]
        squares = gathered[:, chunks : 2 * chunks]
        counts = gathered[:, 2 * chunks :]
        count = jnp.sum(counts, axis=0)
        total = jnp.sum(sums, axis=0)
        mean = total / jnp.maximum(count, 1.0)
        shift = sums / jnp.maximum(counts, 1.0) - mean[None]
        return total, jnp.sum(squares, axis=0) + jnp.sum(counts * shift * shift, axis=0), count, mean

    gather_first(stat_a, recv_a, 9)
    total, squares, count, mean = merged(recv_a[...])
    stat_b[:chunks] = total
    stat_b[chunks : 2 * chunks] = squares
    stat_b[2 * chunks :] = count
    gather_second(stat_b, recv_b, 10)
    total, squares, count, mean = merged(recv_b[...])
    tot_ref[:chunks] = mean
    tot_ref[chunks : 2 * chunks] = lax.rsqrt(squares / count + EPSILON)
    tot_ref[2 * chunks : 3 * chunks] = 1.0 / count

    @pl.loop(0, chunks)
    def _(chunk):
        columns = column(chunk)
        mean = tot_ref[pl.ds(chunk, 1)]
        inverse = tot_ref[pl.ds(chunks + chunk, 1)]
        normed = (conv_ref[:, columns] - mean) * inverse
        conv_ref[:, columns] = normed
        act = normed * gain_ref[:, columns] + shift_ref[:, columns]
        gate = 1.0 / (1.0 + jnp.exp(-act))
        grad_out = jnp.where(live(mid, -16), cot_ext[:, columns].astype(F32), 0.0)
        grad_act = grad_out * gate * (1.0 + act * (1.0 - gate))
        ga_ref[:, columns] = grad_act
        own = grad_act[16 : 16 + ROWS]
        stat_c[pl.ds(chunk, 1)] = jnp.sum(own * normed[16 : 16 + ROWS], axis=0, keepdims=True)
        stat_c[pl.ds(chunks + chunk, 1)] = jnp.sum(own, axis=0, keepdims=True)
        gated = (act * gate)[16 : 16 + ROWS]
        hidden = hid_ref[HALO : HALO + ROWS, columns]
        out_ref[:, columns] = jnp.where(live(ROWS, 0), hidden + gated, 0.0).astype(BF16)

    gather_first(stat_c, recv_c, 11)
    stat_d[...] = jnp.sum(recv_c[...], axis=0)
    gather_second(stat_d, recv_d, 12)
    sums_ref[...] = jnp.sum(recv_d[...], axis=0)

    @pl.loop(0, chunks)
    def _(chunk):
        columns = column(chunk)
        inverse = tot_ref[pl.ds(chunks + chunk, 1)]
        per_count = tot_ref[pl.ds(2 * chunks + chunk, 1)]
        gain_sum = sums_ref[pl.ds(chunk, 1)] * per_count
        shift_sum = sums_ref[pl.ds(chunks + chunk, 1)] * per_count
        grad_act = ga_ref[:, columns]
        grad_conv = (inverse * gain_ref[:, columns]) * (grad_act - (shift_sum + conv_ref[:, columns] * gain_sum))
        grad_conv = jnp.where(live(mid, -16), grad_conv, 0.0)
        ga_ref[:, columns] = grad_conv
        total = cot_ext[16 : 16 + ROWS, columns].astype(F32)
        for low in range(8):
            moved = shifted(grad_conv, low)
            for high_part in range(4):
                tap = 31 - (8 * high_part + low)
                if 0 <= tap < KERNEL:
                    total = total + taps_ref[tap : tap + 1, columns] * moved[8 * high_part : 8 * high_part + ROWS]
        ginp_ref[:, columns] = jnp.where(live(ROWS, 0), total, 0.0).astype(BF16)

    @pl.loop(0, heads // 2)
    def _(pair):
        rows = pl.ds(pl.multiple_of(pair * 128, 128), 128)
        grad_context = dot(ginp_ref[...], w_ref[rows], ((1,), (1,))).astype(BF16).astype(F32)
        even, odd = pack_pair(grad_context)
        do_send[2 * pair] = even.astype(BF16)
        do_send[2 * pair + 1] = odd.astype(BF16)

    to_heads(do_send, do_recv, 13, 14)

    own_context = jnp.transpose(ctx_ref[HALO : HALO + ROWS].astype(F32)).astype(BF16)

    @pl.loop(0, channels // 256)
    def _(chunk):
        columns = pl.ds(pl.multiple_of(chunk * 256, 256), 256)
        terms = dot(own_context, ginp_ref[:, columns]).astype(BF16)
        wsend[:, :, :, columns] = terms.reshape(2, chips, 16, 256)

    wsend[:, :, :, channels:] = jnp.zeros((2, chips, 16, 128), BF16)

    @pl.loop(0, chunks)
    def _(chunk):
        columns = column(chunk)
        grad_conv = ga_ref[16 : 16 + ROWS, columns]
        hidden = hid_ref[16:, columns]
        found = [None] * 32
        for low in range(8):
            moved = shifted(hidden, low)
            for high_part in range(4):
                tap = 8 * high_part + low - 1
                if 0 <= tap < KERNEL:
                    terms = grad_conv * moved[8 * high_part : 8 * high_part + ROWS]
                    found[tap] = jnp.sum(terms, axis=0, keepdims=True)
        found[31] = jnp.zeros((1, 128), F32)
        stacked = jnp.concatenate(found, axis=0).astype(BF16)
        wsend[0, pl.ds(chunk, 1), :, channels:] = stacked[:16].reshape(1, 16, 128)
        wsend[1, pl.ds(chunk, 1), :, channels:] = stacked[16:].reshape(1, 16, 128)

    stage0 = remote(wsend.at[other], g0, send.at[15], recv.at[15], partner)
    stage0.start()

    drain(do_recv, recv.at[13])
    for index in range(heads):
        rows = slice(ROWS * index, ROWS * index + ROWS)
        scaled = (unpack_high(do_recv[index].astype(F32)) * linv[rows]).astype(BF16)
        docl[rows] = scaled
        scaled = scaled.astype(F32)
        delta = jnp.sum(ctxh[rows] * scaled, axis=1, keepdims=True)
        first = delta.astype(BF16).astype(F32)
        rest = delta - first
        lane = lax.broadcasted_iota(jnp.int32, scaled.shape, 1)
        doaug[rows] = jnp.where(lane == 0, -first, jnp.where(lane == 1, -rest, scaled)).astype(BF16)

    dqt[...] = jnp.zeros_like(dqt)

    def part_copy(turn):
        rows = pl.ds(pl.multiple_of(turn * KEY_BLOCK, KEY_BLOCK), KEY_BLOCK)
        return remote(dsend.at[rows], precv.at[rows], part_send.at[turn], part_recv.at[turn], partner)

    def stage1():
        stage0.wait_recv()

        @pl.loop(0, chips)
        def _(i):
            gs1[i] = (wsend[core, i].astype(F32) + g0[i].astype(F32)).astype(BF16)

        g1[chip] = gs1[chip]

        @pl.loop(1, chips)
        def _(d):
            peer = (chip + d) % chips
            remote(gs1.at[peer], g1.at[chip], send.at[16], recv.at[16], (z, peer * 2 + core)).start()

    def stage2():
        drain(g1.at[pl.ds(0, chips - 1)], recv.at[16])
        total = g1[0].astype(F32)
        for i in range(1, chips):
            total = total + g1[i].astype(F32)
        total = total.astype(BF16)
        gs2[...] = total
        g2[z] = total

        @pl.loop(1, depth)
        def _(d):
            remote(gs2, g2.at[z], send.at[17], recv.at[17], ((z + d) % depth, me)).start()

    def stage3():
        drain(g2.at[pl.ds(0, depth - 1)], recv.at[17])
        total = g2[0].astype(F32)
        for i in range(1, depth):
            total = total + g2[i].astype(F32)
        gfin_ref[core, chip] = total.astype(BF16)

        @pl.loop(1, chips)
        def _(d):
            peer = (chip + d) % chips
            piece = gfin_ref.at[core, chip]
            remote(piece, piece, send.at[18], recv.at[18], (z, peer * 2 + core)).start()

    def stage4_copy():
        piece = gfin_ref.at[core]
        return remote(piece, piece, send.at[19], recv.at[19], partner)

    def stage4():
        drain(gfin_ref.at[core, pl.ds(0, chips - 1)], recv.at[18])
        stage4_copy().start()

    steps = 2 * half_blocks

    @pl.loop(0, steps)
    def _(step):
        half = jnp.where(step < half_blocks, other, core)
        turn = step % half_blocks
        start = pl.multiple_of(half * half_keys + turn * KEY_BLOCK, KEY_BLOCK)
        rows = pl.ds(start, KEY_BLOCK)
        turn_rows = pl.ds(pl.multiple_of(turn * KEY_BLOCK, KEY_BLOCK), KEY_BLOCK)
        terms = jnp.zeros((KEY_BLOCK, 128), F32)
        for block in range(query_blocks):
            part = slice(block * QUERY_BLOCK, (block + 1) * QUERY_BLOCK)
            weights = pt[rows, part]
            grads = dot(v1[rows], doaug[part], ((1,), (1,))).astype(BF16)
            scores = weights * grads
            terms = terms + dot(scores, qcl[part]) + dot(weights, docl[part])
            dqt[:, part] += dot(kt[:, rows], scores)
        rbuf[...] = terms

        @pl.when(step < half_blocks)
        def _():
            dsend[turn_rows] = rbuf[...].astype(BF16)
            part_copy(turn).start()

        @pl.when(step >= half_blocks)
        def _():
            part_copy(turn).wait_recv()
            osend[turn_rows] = (rbuf[...] + precv[turn_rows].astype(F32)).astype(BF16)
            for i in range(KEY_BLOCK // ROWS):
                to = turn * (KEY_BLOCK // ROWS) + i
                source = osend.at[pl.ds(pl.multiple_of(to * ROWS, ROWS), ROWS)]

                @pl.when(to == chip)
                def _():
                    pltpu.make_async_copy(source, kvrecv.at[chip], recv.at[20]).start()

                @pl.when(to != chip)
                def _():
                    remote(source, kvrecv.at[chip], own_sem, recv.at[20], (z, to * 2 + core)).start()

        for number, stage in enumerate((stage1, stage2, stage3)):

            @pl.when(step == (number * steps) // 4 + max(steps // 4 - 1, 0))
            def _(stage=stage):
                stage()

    @pl.loop(0, query_blocks)
    def _(block):
        part = pl.ds(pl.multiple_of(block * QUERY_BLOCK, QUERY_BLOCK), QUERY_BLOCK)
        turned = dqt[:, part]
        turned = jnp.transpose(jnp.concatenate([turned, jnp.zeros_like(turned)], axis=0))
        half_part = pl.ds(pl.multiple_of(block * QUERY_BLOCK // 2, QUERY_BLOCK // 2), QUERY_BLOCK // 2)
        dq_send[half_part] = pack_low(turned).astype(BF16)

    for i in range(heads):
        source = dq_send.at[pl.ds(64 * i, 64)]
        target = dq_recv.at[my_head]

        @pl.when(owner_of(i) == me)
        def _(source=source, target=target):
            pltpu.make_async_copy(source, target, recv.at[21]).start()

        @pl.when(owner_of(i) != me)
        def _(source=source, target=target, i=i):
            remote(source, target, dq_sem.at[i], recv.at[21], (z, owner_of(i))).start()

    stage4()

    drain(kvrecv, recv.at[20])
    for pair in range(heads // 2):
        columns = slice(128 * pair, 128 * pair + 128)
        even = kvrecv[2 * pair].astype(F32) + kvrecv[2 * pair + heads].astype(F32)
        odd = kvrecv[2 * pair + 1].astype(F32) + kvrecv[2 * pair + 1 + heads].astype(F32)
        low = low_lanes(even.shape)
        gk_ref[:, columns] = jnp.where(low, even, roll64(odd)).astype(BF16)
        gv_ref[:, columns] = jnp.where(low, roll64(even), odd).astype(BF16)

    drain(dq_recv, recv.at[21])
    for pair in range(heads // 2):
        gq_ref[:, 128 * pair : 128 * pair + 128] = unpack_pair(
            dq_recv[2 * pair].astype(F32), dq_recv[2 * pair + 1].astype(F32)
        ).astype(BF16)

    drain(kvbuf.at[pl.ds(0, (chips - 1) * ROWS)], send.at[0])
    to_heads_done(qpk, 1, 2)
    for copy in halo_copies:
        copy.wait_send()
    forward.wait_send()
    for index, (i, start, count, to) in enumerate(moves):

        @pl.when(owner_of(i) != me)
        def _(index=index, start=start, count=count):
            drain(ctx_send.at[pl.ds(start, count)], ctx_sem.at[index])

    drain(recv_a.at[pl.ds(0, 2 * depth - 1)], send.at[9])
    drain(recv_b.at[pl.ds(0, chips - 1)], send.at[10])
    drain(recv_c.at[pl.ds(0, 2 * depth - 1)], send.at[11])
    drain(recv_d.at[pl.ds(0, chips - 1)], send.at[12])
    to_heads_done(do_recv, 13, 14)
    stage0.wait_send()
    drain(g1.at[pl.ds(0, chips - 1)], send.at[16])
    drain(g2.at[pl.ds(0, depth - 1)], send.at[17])
    drain(gfin_ref.at[core, pl.ds(0, chips - 1)], send.at[18])

    @pl.loop(0, half_blocks)
    def _(turn):
        part_copy(turn).wait_send()

    drain(kvrecv.at[pl.ds(0, chips - 1)], own_sem)
    for i in range(heads):

        @pl.when(owner_of(i) != me)
        def _(i=i):
            drain(dq_send.at[pl.ds(64 * i, 64)], dq_sem.at[i])

    last = stage4_copy()
    last.wait_send()
    rest = gfin_ref.at[other]
    drain(rest, recv.at[19])


def shards(
    depth,
    query_rows,
    key_rows,
    value_rows,
    inputs,
    lengths,
    out_weight,
    taps,
    norm_gain,
    norm_shift,
    cotangent,
):
    seq = lax.axis_size("seq")
    heads = seq // 4
    chips = seq // 2
    width = query_rows.shape[2]
    channels = inputs.shape[2]
    chunks = channels // 128
    queries = ROWS * heads
    keys = seq * ROWS
    ext = ROWS + 2 * HALO
    mid = ROWS + 32
    padded = channels + 128
    vmem = pltpu.VMEM
    scratch = [
        vmem((heads, ROWS, 128), BF16),
        vmem((heads, 64, 128), BF16),
        vmem((keys, 128), BF16),
        vmem((heads, 64, 128), BF16),
        vmem((keys, 128), BF16),
        vmem((keys, 128), BF16),
        vmem((64, keys), BF16),
        vmem((128, keys), BF16),
        vmem((queries, 128), BF16),
        vmem((queries, 128), BF16),
        vmem((2, keys, QUERY_BLOCK), F32),
        vmem((keys, queries), BF16),
        vmem((queries, 128), F32),
        vmem((queries, 128), F32),
        vmem((queries // 2, 128), BF16),
        vmem((heads, ext // 2, 128), BF16),
        vmem((ext, channels), BF16),
        vmem((mid, channels), BF16),
        vmem((width, channels), BF16),
        vmem((KERNEL, channels), F32),
        vmem((ext, width), BF16),
        vmem((ext, channels), F32),
        vmem((mid, channels), F32),
        vmem((mid, channels), F32),
        vmem((3 * chunks, 128), F32),
        vmem((3 * chunks, 128), F32),
        vmem((2 * depth, 3 * chunks, 128), F32),
        vmem((chips, 3 * chunks, 128), F32),
        vmem((2 * chunks, 128), F32),
        vmem((2 * depth, 2 * chunks, 128), F32),
        vmem((2 * chunks, 128), F32),
        vmem((chips, 2 * chunks, 128), F32),
        vmem((3 * chunks, 128), F32),
        vmem((heads, 64, 128), BF16),
        vmem((heads, 64, 128), BF16),
        vmem((queries, 128), BF16),
        vmem((queries, 128), BF16),
        vmem((KEY_BLOCK, 128), F32),
        vmem((64, queries), F32),
        vmem((keys // 2, 128), BF16),
        vmem((keys // 2, 128), BF16),
        vmem((keys // 2, 128), BF16),
        vmem((chips, ROWS, 128), BF16),
        vmem((queries // 2, 128), BF16),
        vmem((heads, 64, 128), BF16),
        vmem((2, chips, 16, padded), BF16),
        vmem((chips, 16, padded), BF16),
        vmem((chips, 16, padded), BF16),
        vmem((chips, 16, padded), BF16),
        vmem((16, padded), BF16),
        vmem((depth, 16, padded), BF16),
        pltpu.SemaphoreType.DMA((4,)),
        pltpu.SemaphoreType.DMA((22,)),
        pltpu.SemaphoreType.DMA((22,)),
        pltpu.SemaphoreType.DMA((heads + 2,)),
        pltpu.SemaphoreType.DMA((heads,)),
        pltpu.SemaphoreType.DMA((keys // 2 // KEY_BLOCK,)),
        pltpu.SemaphoreType.DMA((keys // 2 // KEY_BLOCK,)),
        pltpu.SemaphoreType.DMA,
    ]
    in_vmem = pl.BlockSpec(memory_space=pltpu.VMEM)
    anywhere = pl.BlockSpec(memory_space=pl.ANY)
    output, grad_inputs, grad_query, grad_key, grad_value, packed, sums = pl.pallas_call(
        functools.partial(kernel, heads, seq, depth),
        out_shape=(
            jax.ShapeDtypeStruct((ROWS, channels), BF16),
            jax.ShapeDtypeStruct((ROWS, channels), BF16),
            jax.ShapeDtypeStruct((ROWS, width), BF16),
            jax.ShapeDtypeStruct((ROWS, width), BF16),
            jax.ShapeDtypeStruct((ROWS, width), BF16),
            jax.ShapeDtypeStruct((2, chips, 16, padded), BF16),
            jax.ShapeDtypeStruct((2 * chunks, 128), F32),
        ),
        in_specs=[pl.BlockSpec(memory_space=pltpu.SMEM), in_vmem, in_vmem, in_vmem]
        + [anywhere] * 4
        + [in_vmem] * 2,
        out_specs=(in_vmem,) * 7,
        scratch_shapes=scratch,
        compiler_params=pltpu.CompilerParams(
            collective_id=0, has_side_effects=True, vmem_limit_bytes=60 * 1024 * 1024
        ),
    )(
        lengths,
        query_rows[0],
        key_rows[0],
        value_rows[0],
        inputs[0],
        cotangent[0],
        out_weight,
        taps,
        norm_gain[None],
        norm_shift[None],
    )
    grad_out_weight = packed[..., :channels].reshape(width, channels).astype(F32)
    tap_terms = packed[:, :chunks, :, channels:].astype(F32)
    grad_kernel = jnp.transpose(tap_terms, (0, 2, 1, 3)).reshape(32, channels)[:KERNEL]
    return (
        output[None],
        grad_inputs[None],
        grad_query[None],
        grad_key[None],
        grad_value[None],
        grad_out_weight,
        grad_kernel,
        sums[:chunks].reshape(channels),
        sums[chunks:].reshape(channels),
    )


def solution(mesh):
    rows = P("dp", "seq", None)
    return jax.shard_map(
        functools.partial(shards, mesh.shape["dp"]),
        mesh=mesh,
        in_specs=(rows, rows, rows, rows, P("dp"), P(), P(), P(), P(), rows),
        out_specs=(rows, rows, rows, rows, rows, P(), P(), P(), P()),
        check_vma=False,
    )
```

time: 899 us -> 125 us (0.14)
  waiting for transfers between devices: 436 us -> 0 us
  blocking collectives: 225 us -> 0 us
  Pallas kernels: 0 us -> 114 us
  local copies, waits for them, and re-layouts: 103 us -> 6.84 us
  matrix products: 59.2 us -> 0 us
  other arithmetic: 27.8 us -> 2.3 us
  loops' own time: 16.8 us -> 0 us
  between operations: 15.3 us -> 1.35 us
  starting transfers between devices: 11.1 us -> 0 us
    psum x1 -> x0, waiting for transfers between devices: 267 us -> none  [shards(): lax.psum((kernel_terms, weight_terms), ('dp', 'seq'))]
    psum x3 -> x0, blocking collectives: 225 us -> none  [the longest x1 78.9 us: shards(): lax.psum((local_count, jnp.sum(masked_conv, axis=0)), ('dp', 'seq'))]
    pallas_call x0 -> x1, Pallas kernels: none -> 114 us  [shards(): pl.pallas_call(functools.partial(kernel, heads, seq, depth), out_shape=(j...]
    reduce_scatter x1 -> x0, waiting for transfers between devices: 91.5 us -> none  [shards(): lax.psum_scatter(key_terms_all.astype(jnp.bfloat16), 'seq', scatter_dimen...]
    all_gather x2 -> x0, waiting for transfers between devices: 74.4 us -> none  [the longest x1 53.4 us: shards(): lax.all_gather(own_keys, 'seq', axis=0, tiled=True)]
    dynamic_slice x72 -> x0, local copies, waits for them, and re-layouts: 61.3 us -> none  [the longest x16 18.8 us: compute(): key_block = lax.dynamic_slice_in_dim(all_keys, block_start, block_rows, 0)]
    dot_general x59 -> x0, matrix products: 59.2 us -> none  [the longest x16 16.5 us: head_scores(): jnp.einsum('qhd,khd->hqk', split_heads(queries), split_heads(key_block),...]
    another operation x3 -> x0, loops' own time: 16.8 us -> none  [the longest x2 11.2 us: over_blocks(): lax.scan(over_advance, initial, jnp.arange(block_count, dtype=jnp.int32))]
  transfers between devices with their start and end apart: 8 -> 0, of which waited for: 5 -> 0; matrix products, arithmetic and copies ran while one was open for 5% -> 0% of each run, Pallas kernels for 0% -> 0%
where the time goes in v1:
time: 125 us
  Pallas kernels  114 us (91%)
  local copies, waits for them, and re-layouts  6.84 us (5%)
  other arithmetic  2.3 us (2%)
  between operations  1.35 us (1%)
    pallas_call x1, Pallas kernels, shards(): pl.pallas_call(functools.partial(kernel, heads, seq, depth), out_shape=(j...  114 us
    unnamed x16, local copies, waits for them, and re-layouts  3.4 us

profile of v1, /device:TPU:1, one launch (start us, length us, event | category | flops | bytes accessed | tf_op | source)
XLA Modules:
  0.0 124.6 jit_solution(10177164957450165442)
XLA Ops:
  1.3 114.1 %shard_map.169 = (bf16[128,1024]{1,0:T(8,128)(2,1)}, bf16[128,1024]{1,0:T(8,128)(2,1)}, bf16[128,512]{1,0:T(8,128)(2,1)}, bf16[128,512]{1,0:T(8,128)(2,1)}, bf16...) custom-call(s32[1]{0:T(128)S(6)} %copy.28.length_ref, bf16[128,512]{1,0:T(8,128)(2,1)} %bitcast.32, ...), custom_call_target="tpu_custom_call" | custom-call | tf_op jit(solution)/shard_map/pallas_call | solution.py:850
  115.4 1.3 %slice_bitcast_fusion.1 = (f32[1024]{0:T(1024)}, f32[1024]{0:T(1024)}) fusion(f32[16,128]{1,0:T(8,128)} %get-tuple-element.22), kind=kLoop, calls=%fused_computation.4 | loop fusion | bytes 16384 | tf_op jit(solution)/shard_map/reshape | solution.py:893
  116.7 0.8 slice_bitcast_fusion
  117.6 1.3 %slice.18 = bf16[2,16,16,1024]{3,2,1,0:T(8,128)(2,1)S(1)} slice(bf16[2,16,16,1152]{3,2,1,0:T(8,128)(2,1)} %get-tuple-element.21), slice={[0:2], [0:16], [0:16], [0:1024]} | slice | bytes 2097152 | tf_op jit(solution)/shard_map/slice | solution.py:881
  118.9 0.0 copy-start.1
  118.9 0.0 copy-start
  118.9 0.7 slice_convert_fusion
  119.6 0.0 copy-start.4
  119.6 0.0 copy-start.3
  119.6 0.0 copy-start.2
  119.6 1.6 %bitcast_convert_fusion = f32[512,1024]{1,0:T(8,128)} fusion(bf16[2,16,16,1024]{3,2,1,0:T(8,128)(2,1)S(1)} %slice.18), kind=kLoop, calls=%fused_computation | loop fusion | flops 524288 | bytes 3145728 | tf_op jit(solution)/shard_map/convert_element_type | solution.py:881
  121.2 0.0 copy-done.1
  121.2 0.7 copy.29
  121.9 0.0 copy-done
  121.9 0.7 copy.30
  122.7 0.0 copy-done.4
  122.7 0.7 copy.31
  123.3 0.0 copy-done.3
  123.3 0.7 copy.32
  124.0 0.0 copy-done.2
  124.0 0.7 copy.33
  (2 shorter events, 0.0 us)
Async XLA Ops:
  118.9 2.4 %copy-start.1 = (bf16[128,1024]{1,0:T(8,128)(2,1)S(1)}, bf16[128,1024]{1,0:T(8,128)(2,1)}, u32[]{:S(2)}) copy-start(bf16[128,1024]{1,0:T(8,128)(2,1)} %get-tuple-element.16) | copy-start | bytes 786436
  118.9 3.1 %copy-start = (bf16[128,1024]{1,0:T(8,128)(2,1)S(1)}, bf16[128,1024]{1,0:T(8,128)(2,1)}, u32[]{:S(2)}) copy-start(bf16[128,1024]{1,0:T(8,128)(2,1)} %get-tuple-element.17) | copy-start | bytes 786436
  119.6 3.1 %copy-start.4 = (bf16[128,512]{1,0:T(8,128)(2,1)S(1)}, bf16[128,512]{1,0:T(8,128)(2,1)}, u32[]{:S(2)}) copy-start(bf16[128,512]{1,0:T(8,128)(2,1)} %get-tuple-element.18) | copy-start | bytes 393220
  119.6 3.7 %copy-start.3 = (bf16[128,512]{1,0:T(8,128)(2,1)S(1)}, bf16[128,512]{1,0:T(8,128)(2,1)}, u32[]{:S(2)}) copy-start(bf16[128,512]{1,0:T(8,128)(2,1)} %get-tuple-element.19) | copy-start | bytes 393220
  119.6 4.4 %copy-start.2 = (bf16[128,512]{1,0:T(8,128)(2,1)S(1)}, bf16[128,512]{1,0:T(8,128)(2,1)}, u32[]{:S(2)}) copy-start(bf16[128,512]{1,0:T(8,128)(2,1)} %get-tuple-element.20) | copy-start | bytes 393220

commit v2 on v1

v2 whole, which is shorter than its diff:
```python
import functools

import jax
import jax.numpy as jnp
from jax import lax
from jax.experimental import pallas as pl
from jax.experimental.pallas import tpu as pltpu
from jax.sharding import PartitionSpec as P

KERNEL = 31
HALF = 15
HEAD_DIM = 64
ROWS = 128
HALO = 32
NEGATIVE = -1e30
EPSILON = 1e-05
PIECES = 3
MESH = pl.DeviceIdType.MESH
F32 = jnp.float32
BF16 = jnp.bfloat16


def roll64(x):
    return pltpu.roll(x, 64, 1)


def low_lanes(shape):
    return lax.broadcasted_iota(jnp.int32, shape, 1) < 64


def split_units(x):
    rows = x.shape[0]
    units = x.reshape(rows // 32, 2, 16, 128)
    return units[:, 0].reshape(rows // 2, 128), units[:, 1].reshape(rows // 2, 128)


def join_units(first, second):
    rows = first.shape[0]
    first = first.reshape(rows // 16, 1, 16, 128)
    second = second.reshape(rows // 16, 1, 16, 128)
    return jnp.concatenate([first, second], axis=1).reshape(2 * rows, 128)


def pack_pair(x):
    first, second = split_units(x)
    low = low_lanes(first.shape)
    even = jnp.where(low, first, roll64(second))
    odd = jnp.where(low, roll64(first), second)
    return even, odd


def unpack_pair(even, odd):
    low = low_lanes(even.shape)
    return join_units(jnp.where(low, even, roll64(odd)), jnp.where(low, roll64(even), odd))


def unpack_low(packed):
    low = low_lanes(packed.shape)
    return join_units(jnp.where(low, packed, 0.0), jnp.where(low, roll64(packed), 0.0))


def unpack_high(packed):
    low = low_lanes(packed.shape)
    return join_units(jnp.where(low, 0.0, roll64(packed)), jnp.where(low, 0.0, packed))


def pack_low(x):
    first, second = split_units(x)
    return jnp.where(low_lanes(first.shape), first, roll64(second))


def pack_high(x):
    first, second = split_units(x)
    return jnp.where(low_lanes(first.shape), roll64(first), second)


def dot(a, b, dims=((1,), (0,))):
    return lax.dot_general(a, b, (dims, ((), ())), preferred_element_type=F32)


def shifted(x, amount):
    return x if amount == 0 else pltpu.roll(x, x.shape[0] - amount, 0)


def kernel(
    heads,
    seq,
    depth,
    length_ref,
    q_hbm,
    k_hbm,
    v_hbm,
    x_hbm,
    cot_hbm,
    w_hbm,
    taps_hbm,
    gain_hbm,
    shift_hbm,
    out_hbm,
    ginp_hbm,
    gq_hbm,
    gk_hbm,
    gv_hbm,
    gfin_ref,
    sums_ref,
    q_ref,
    k_ref,
    v_ref,
    gain_ref,
    shift_ref,
    out_ref,
    ginp_ref,
    gq_ref,
    gk_ref,
    gv_ref,
    len_send,
    len_recv,
    cmask_ref,
    cgrad_ref,
    cnorm_ref,
    kv_send,
    q_send,
    kvbuf,
    qpk,
    k1,
    v1,
    kt,
    v1t,
    qaug,
    qcl,
    sbuf,
    pt,
    ctxh,
    linv,
    ctx_send,
    ctx_recv,
    x_ext,
    cot_ext,
    w_ref,
    taps_ref,
    ctx_ref,
    hid_ref,
    conv_ref,
    ga_ref,
    stat_a,
    stat_b,
    recv_a,
    recv_b,
    stat_c,
    recv_c,
    stat_d,
    recv_d,
    tot_ref,
    do_send,
    do_recv,
    doaug,
    docl,
    rbuf,
    dqt,
    dsend,
    precv,
    osend,
    kvrecv,
    dq_send,
    dq_recv,
    wsend,
    g0,
    gs1,
    g1,
    gs2,
    g2,
    load_sem,
    send,
    recv,
    ctx_sem,
    dq_sem,
    part_send,
    part_recv,
    own_sem,
    piece_send,
    piece_recv,
    write_sem,
):
    chips = seq // 2
    width = q_ref.shape[1]
    channels = out_ref.shape[1]
    chunks = channels // 128
    queries = ROWS * heads
    half_keys = chips * ROWS
    forward_block = half_keys // 2
    backward_block = half_keys // 4
    query_block = min(queries, 512)
    query_blocks = queries // query_block
    padded = channels + 128
    piece_width = padded // PIECES
    ext = ROWS + 2 * HALO
    mid = ROWS + 32

    z = lax.axis_index("dp")
    me = lax.axis_index("seq")
    chip = me // 2
    core = me % 2
    other = 1 - core
    partner = (z, chip * 2 + other)
    group = (chip // heads) * 2 + core
    my_group = me // heads
    length = length_ref[0]

    def remote(src, dst, send_sem, recv_sem, device):
        return pltpu.make_async_remote_copy(
            src_ref=src, dst_ref=dst, send_sem=send_sem, recv_sem=recv_sem, device_id=device, device_id_type=MESH
        )

    def drain(ref, sem):
        pltpu.make_async_copy(ref, ref, sem).wait()

    pending = {}

    def later(name, ref, sem):
        pending[name] = lambda: drain(ref, sem)

    def settle(*names):
        for name in names or tuple(pending):
            pending.pop(name)()

    barrier = pltpu.get_barrier_semaphore()

    @pl.loop(1, seq)
    def _(d):
        pl.semaphore_signal(barrier, inc=1, device_id=(z, (me + d) % seq), device_id_type=MESH)

    @pl.loop(1, depth)
    def _(d):
        for c in range(2):
            pl.semaphore_signal(
                barrier, inc=1, device_id=((z + d) % depth, chip * 2 + c), device_id_type=MESH
            )

    loads = (
        ("k", k_hbm, k_ref),
        ("v", v_hbm, v_ref),
        ("q", q_hbm, q_ref),
        ("x", x_hbm, x_ext.at[pl.ds(HALO, ROWS)]),
        ("cot", cot_hbm, cot_ext.at[pl.ds(16, ROWS)]),
        ("w", w_hbm, w_ref),
        ("taps", taps_hbm, taps_ref),
        ("gain", gain_hbm, gain_ref),
        ("shift", shift_hbm, shift_ref),
    )
    for index, (name, source, target) in enumerate(loads):
        copy = pltpu.make_async_copy(source, target, load_sem.at[index])
        copy.start()
        pending[name] = copy.wait

    len_send[...] = jnp.full((8, 128), length.astype(F32), F32)
    settle("k", "v", "q")
    for pair in range(heads // 2):
        columns = slice(128 * pair, 128 * pair + 128)
        kp = k_ref[:, columns].astype(F32)
        vp = v_ref[:, columns].astype(F32)
        low = low_lanes(kp.shape)
        kv_send[2 * pair] = jnp.where(low, kp, roll64(vp)).astype(BF16)
        kv_send[2 * pair + 1] = jnp.where(low, roll64(kp), vp).astype(BF16)
        even, odd = pack_pair(q_ref[:, columns].astype(F32))
        q_send[2 * pair] = even.astype(BF16)
        q_send[2 * pair + 1] = odd.astype(BF16)

    pl.semaphore_wait(barrier, seq - 1 + 2 * (depth - 1))

    def kv_slot(d):
        return kvbuf.at[pl.ds(pl.multiple_of(core * half_keys + d * ROWS, ROWS), ROWS)]

    def send_keys(first, last, index):
        @pl.loop(first, last)
        def _(d):
            peer = (chip + d) % chips
            remote(kv_send.at[peer % heads], kv_slot(d), send.at[index], recv.at[index], (z, peer * 2 + core)).start()

    def quarter(half, index):
        return kvbuf.at[
            pl.ds(pl.multiple_of(half * half_keys + index * forward_block, forward_block), forward_block)
        ]

    some = chips // 2
    pltpu.make_async_copy(kv_send.at[chip % heads], kv_slot(0), recv.at[0]).start()
    send_keys(1, some, 0)
    later("keys 0 in", quarter(core, 0), recv.at[0])
    later("keys 0 out", kvbuf.at[pl.ds(0, (some - 1) * ROWS)], send.at[0])

    def head_device(head):
        return ((my_group // 2) * heads + head) * 2 + my_group % 2

    def to_heads(source, target, index, self_index):
        head = chip % heads
        slot = me % heads
        mine = head_device(head) == me

        @pl.when(mine)
        def _():
            pltpu.make_async_copy(source.at[head], target.at[slot], recv.at[index]).start()

        @pl.when(jnp.logical_not(mine))
        def _():
            remote(
                source.at[head], target.at[slot], send.at[self_index], recv.at[index], (z, head_device(head))
            ).start()

        @pl.loop(1, heads)
        def _(d):
            to = (chip + d) % heads
            remote(
                source.at[to], target.at[slot], send.at[index], recv.at[index], (z, head_device(to))
            ).start()

        def own_done():
            @pl.when(jnp.logical_not(mine))
            def _():
                drain(target.at[0], send.at[self_index])

        later(f"heads {index} in", target, recv.at[index])
        later(f"heads {index} out", target.at[pl.ds(0, heads - 1)], send.at[index])
        pending[f"heads {index} own"] = own_done

    to_heads(q_send, qpk, 1, 2)

    send_keys(some, chips, 22)
    later("keys 1 in", quarter(core, 1), recv.at[22])
    later("keys 1 out", kvbuf.at[pl.ds(0, some * ROWS)], send.at[22])

    len_recv[z] = len_send[...]

    @pl.loop(1, depth)
    def _(d):
        remote(len_send, len_recv.at[z], send.at[23], recv.at[23], ((z + d) % depth, me)).start()

    later("lengths in", len_recv.at[pl.ds(0, depth - 1)], recv.at[23])
    later("lengths out", len_recv.at[pl.ds(0, depth - 1)], send.at[23])

    after = (z, (me + 1) % seq)
    before = (z, (me + seq - 1) % seq)
    settle("x", "cot")
    halo_copies = (
        remote(x_ext.at[pl.ds(ROWS, HALO)], x_ext.at[pl.ds(0, HALO)], send.at[3], recv.at[3], after),
        remote(x_ext.at[pl.ds(HALO, HALO)], x_ext.at[pl.ds(HALO + ROWS, HALO)], send.at[4], recv.at[4], before),
        remote(cot_ext.at[pl.ds(ROWS, 16)], cot_ext.at[pl.ds(0, 16)], send.at[5], recv.at[5], after),
        remote(cot_ext.at[pl.ds(16, 16)], cot_ext.at[pl.ds(16 + ROWS, 16)], send.at[6], recv.at[6], before),
    )
    for index, copy in enumerate(halo_copies):
        copy.start()
        pending[f"halo {index} in"] = copy.wait_recv
        pending[f"halo {index} out"] = copy.wait_send

    def prepare_keys(half, index):
        rows_at_once = min(forward_block, 512)

        @pl.loop(0, forward_block // rows_at_once)
        def _(part):
            first = index * forward_block + part * rows_at_once
            rows = pl.ds(pl.multiple_of(half * half_keys + first, rows_at_once), rows_at_once)
            kv = kvbuf[rows].astype(F32)
            lane = lax.broadcasted_iota(jnp.int32, kv.shape, 1)
            row = lax.broadcasted_iota(jnp.int32, kv.shape, 0) + first
            source = chip - (row >> 7)
            source = jnp.where(source < 0, source + chips, source)
            frame = (source * 2 + half) * ROWS + (row & 127)
            bias = jnp.where(jnp.logical_and(lane == 64, frame >= length), NEGATIVE, 0.0)
            keyed = jnp.where(lane < 64, kv, bias)
            valued = jnp.where(lane < 64, 1.0, kv)
            k1[rows] = keyed.astype(BF16)
            v1[rows] = valued.astype(BF16)
            kt[:, rows] = jnp.transpose(kv)[:64].astype(BF16) * BF16(0.125)
            v1t[:, rows] = jnp.transpose(valued).astype(BF16)

    factor = 0.125 * 1.4426950408889634

    def block_rows(block):
        return pl.ds(pl.multiple_of(block * forward_block, forward_block), forward_block)

    def scores_step(part, block, highest):
        scores = dot(
            k1[block_rows(block)], qaug[part * query_block : (part + 1) * query_block], ((1,), (1,))
        )
        sbuf[part % 2, block_rows(block)] = scores
        return jnp.maximum(highest, jnp.max(scores.reshape(forward_block // 8, 8, query_block), axis=0))

    def weights_step(part, block, highest, total):
        rows = block_rows(block)
        weights = jnp.exp2((sbuf[part % 2, rows] - highest) * factor).astype(BF16)
        pt[rows, part * query_block : (part + 1) * query_block] = weights
        return total + dot(v1t[:, rows], weights)

    def context_finish(part, total):
        turned = jnp.transpose(total)
        low = low_lanes(turned.shape)
        inverse = 1.0 / jnp.where(low, 1.0, roll64(turned))
        context = jnp.where(low, 0.0, turned * inverse).astype(BF16).astype(F32)
        rows = slice(part * query_block, (part + 1) * query_block)
        linv[rows] = inverse
        ctxh[rows] = context
        half_rows = slice(part * query_block // 2, (part + 1) * query_block // 2)
        ctx_send[half_rows] = pack_high(context).astype(BF16)

    high = jnp.full((8, query_block), NEGATIVE, F32)
    for index in range(2):
        settle(f"keys {index} in")
        forward = remote(
            quarter(core, index), quarter(core, index), send.at[7 + 17 * index], recv.at[7 + 17 * index], partner
        )
        forward.start()
        later(f"forward {index} in", quarter(other, index), recv.at[7 + 17 * index])
        pending[f"forward {index} out"] = forward.wait_send
        prepare_keys(core, index)
        if index == 0:
            settle("heads 1 in")
            for slot in range(heads):
                rows = slice(ROWS * slot, ROWS * slot + ROWS)
                part = unpack_low(qpk[slot].astype(F32))
                lane = lax.broadcasted_iota(jnp.int32, part.shape, 1)
                qcl[rows] = (part * 0.125).astype(BF16)
                qaug[rows] = jnp.where(lane == 64, 1.0, part).astype(BF16)
        high = scores_step(0, core * 2 + index, high)
    for index in range(2):
        settle(f"forward {index} in")
        prepare_keys(other, index)
        high = scores_step(0, other * 2 + index, high)

    start_high = jnp.full((8, query_block), NEGATIVE, F32)
    start_total = jnp.zeros((128, query_block), F32)
    for part in range(query_blocks):
        highest = jnp.max(high, axis=0, keepdims=True)
        if part + 1 < query_blocks:

            def both(b, carried, part=part, highest=highest):
                h, t = carried
                return scores_step(part + 1, b, h), weights_step(part, b, highest, t)

            high, total = lax.fori_loop(0, 4, both, (start_high, start_total))
        else:
            total = lax.fori_loop(
                0, 4, lambda b, t, part=part, highest=highest: weights_step(part, b, highest, t), start_total
            )
        context_finish(part, total)

    my_head = chip % heads
    moves = [(-1, 0, 16, 80), (0, 0, 80, 16)]
    moves += [(i, 64 * i - 16, 96, 0) for i in range(1, heads - 1)]
    moves += [(heads - 1, 64 * (heads - 1) - 16, 80, 0), (heads, 64 * heads - 16, 16, 0)]

    def owner_of(i):
        return (group * heads + i + seq) % seq

    for index, (i, start, count, to) in enumerate(moves):
        source = ctx_send.at[pl.ds(start, count)]
        target = ctx_recv.at[my_head, pl.ds(to, count)]

        @pl.when(owner_of(i) == me)
        def _(source=source, target=target):
            pltpu.make_async_copy(source, target, recv.at[8]).start()

        @pl.when(owner_of(i) != me)
        def _(source=source, target=target, i=i, index=index):
            remote(source, target, ctx_sem.at[index], recv.at[8], (z, owner_of(i))).start()

        def sent(source=source, i=i, index=index):
            @pl.when(owner_of(i) != me)
            def _():
                drain(source, ctx_sem.at[index])

        pending[f"context {index}"] = sent

    def live(rows, first):
        frame = me * ROWS + first + lax.broadcasted_iota(jnp.int32, (rows, 128), 0)
        return jnp.logical_and(frame >= 0, frame < length)

    def column(chunk):
        return pl.ds(pl.multiple_of(chunk * 128, 128), 128)

    def turned_convolution(rows, columns):
        total = jnp.zeros((ROWS, 128), F32)
        for low in range(8):
            moved = shifted(rows, low)
            for high_part in range(4):
                tap = 31 - (8 * high_part + low)
                if 0 <= tap < KERNEL:
                    total = total + taps_ref[tap : tap + 1, columns] * moved[8 * high_part : 8 * high_part + ROWS]
        return total

    settle("w", "taps", "gain", "shift")

    @pl.loop(0, chunks)
    def _(chunk):
        columns = column(chunk)
        cmask_ref[:, columns] = turned_convolution(jnp.where(live(mid, -16), 1.0, 0.0), columns)

    settle(*(f"halo {index} in" for index in range(4)))
    drain(ctx_recv, recv.at[8])

    for pair in range(heads // 2):
        ctx_ref[:, 128 * pair : 128 * pair + 128] = unpack_pair(
            ctx_recv[2 * pair].astype(F32), ctx_recv[2 * pair + 1].astype(F32)
        ).astype(BF16)

    counted = jnp.clip(length - me * ROWS, 0, ROWS).astype(F32)

    @pl.loop(0, channels // 256)
    def _(chunk):
        columns = pl.ds(pl.multiple_of(chunk * 256, 256), 256)
        hidden = x_ext[:, columns].astype(F32) + dot(ctx_ref[...], w_ref[:, columns])
        mask = live(ext, -HALO)
        mask = jnp.concatenate([mask, mask], axis=1)
        hid_ref[:, columns] = jnp.where(mask, hidden, 0.0).astype(BF16).astype(F32)

    @pl.loop(0, chunks)
    def _(chunk):
        columns = column(chunk)
        hidden = hid_ref[:, columns]
        total = jnp.zeros((mid, 128), F32)
        for low in range(8):
            moved = shifted(hidden, low)
            for high_part in range(4):
                tap = 8 * high_part + low - 1
                if 0 <= tap < KERNEL:
                    total = total + taps_ref[tap : tap + 1, columns] * moved[8 * high_part : 8 * high_part + mid]
        conv_ref[:, columns] = total
        own = total[16 : 16 + ROWS]
        mask = live(ROWS, 0)
        summed = jnp.sum(jnp.where(mask, own, 0.0), axis=0, keepdims=True)
        mean = summed / jnp.maximum(counted, 1.0)
        spread = own - mean
        squares = jnp.sum(jnp.where(mask, spread * spread, 0.0), axis=0, keepdims=True)
        stat_a[pl.ds(chunk, 1)] = summed
        stat_a[pl.ds(chunks + chunk, 1)] = squares

    settle("lengths in")
    lengths = len_recv[:, :1]


    def write(source, target, index):
        copy = pltpu.make_async_copy(source, target, write_sem.at[index])
        copy.start()
        pending[f"write {index}"] = copy.wait

    def gather_first(source, target, index, beside=None):
        slot = z * 2 + core
        target[slot] = source[...]
        remote(source, target.at[slot], send.at[index], recv.at[index], partner).start()

        @pl.loop(1, depth)
        def _(d):
            for c in range(2):
                remote(
                    source, target.at[slot], send.at[index], recv.at[index], ((z + d) % depth, chip * 2 + c)
                ).start()

        later(f"first {index}", target.at[pl.ds(0, 2 * depth - 1)], send.at[index])
        if beside is not None:
            beside()
        drain(target.at[pl.ds(0, 2 * depth - 1)], recv.at[index])

    def gather_second(source, target, index):
        target[chip] = source[...]

        @pl.loop(1, chips)
        def _(d):
            remote(
                source, target.at[chip], send.at[index], recv.at[index], (z, ((chip + d) % chips) * 2 + core)
            ).start()

        later(f"second {index}", target.at[pl.ds(0, chips - 1)], send.at[index])
        drain(target.at[pl.ds(0, chips - 1)], recv.at[index])

    def frames_of(index):
        return jnp.clip(lengths - (index * ROWS).astype(F32), 0.0, float(ROWS))

    def merged(gathered, counts):
        sums = gathered[:, :chunks]
        squares = gathered[:, chunks:]
        count = jnp.sum(counts, axis=0)
        total = jnp.sum(sums, axis=0)
        mean = total / jnp.maximum(count, 1.0)
        shift = sums / jnp.maximum(counts, 1.0) - mean[None]
        return total, jnp.sum(squares, axis=0) + jnp.sum(counts * shift * shift, axis=0), count, mean

    def first_counts():
        both_cores = [frames_of(chip * 2 + c) for c in range(2)]
        return jnp.concatenate([lax.slice_in_dim(both_cores[i % 2], i // 2, i // 2 + 1) for i in range(2 * depth)], axis=0)

    def second_counts():
        per_chip = []
        for i in range(chips):
            first = jnp.clip(lengths - float(2 * i * ROWS), 0.0, float(2 * ROWS))
            per_chip.append(jnp.sum(first, axis=0, keepdims=True))
        return jnp.concatenate(per_chip, axis=0)

    gather_first(stat_a, recv_a, 9)
    total, squares, count, mean = merged(recv_a[...], first_counts())
    stat_b[:chunks] = total
    stat_b[chunks:] = squares
    gather_second(stat_b, recv_b, 10)
    total, squares, count, mean = merged(recv_b[...], second_counts())
    tot_ref[:chunks] = mean
    tot_ref[chunks : 2 * chunks] = lax.rsqrt(squares / count + EPSILON)
    tot_ref[2 * chunks : 3 * chunks] = jnp.broadcast_to(1.0 / count, (chunks, 128))

    @pl.loop(0, chunks)
    def _(chunk):
        columns = column(chunk)
        mean = tot_ref[pl.ds(chunk, 1)]
        inverse = tot_ref[pl.ds(chunks + chunk, 1)]
        normed = (conv_ref[:, columns] - mean) * inverse
        conv_ref[:, columns] = normed
        act = normed * gain_ref[:, columns] + shift_ref[:, columns]
        gate = 1.0 / (1.0 + jnp.exp(-act))
        grad_out = jnp.where(live(mid, -16), cot_ext[:, columns].astype(F32), 0.0)
        grad_act = grad_out * gate * (1.0 + act * (1.0 - gate))
        ga_ref[:, columns] = grad_act
        own = grad_act[16 : 16 + ROWS]
        stat_c[pl.ds(chunk, 1)] = jnp.sum(own * normed[16 : 16 + ROWS], axis=0, keepdims=True)
        stat_c[pl.ds(chunks + chunk, 1)] = jnp.sum(own, axis=0, keepdims=True)
        gated = (act * gate)[16 : 16 + ROWS]
        hidden = hid_ref[HALO : HALO + ROWS, columns]
        out_ref[:, columns] = jnp.where(live(ROWS, 0), hidden + gated, 0.0).astype(BF16)

    def beside():
        write(out_ref, out_hbm, 0)

        @pl.loop(0, chunks)
        def _(chunk):
            columns = column(chunk)
            cgrad_ref[:, columns] = turned_convolution(ga_ref[:, columns], columns)
            cnorm_ref[:, columns] = turned_convolution(
                jnp.where(live(mid, -16), conv_ref[:, columns], 0.0), columns
            )

    gather_first(stat_c, recv_c, 11, beside)
    stat_d[...] = jnp.sum(recv_c[...], axis=0)
    gather_second(stat_d, recv_d, 12)
    sums_ref[...] = jnp.sum(recv_d[...], axis=0)

    @pl.loop(0, chunks)
    def _(chunk):
        columns = column(chunk)
        inverse = tot_ref[pl.ds(chunks + chunk, 1)]
        per_count = tot_ref[pl.ds(2 * chunks + chunk, 1)]
        gain_sum = sums_ref[pl.ds(chunk, 1)] * per_count
        shift_sum = sums_ref[pl.ds(chunks + chunk, 1)] * per_count
        scale = inverse * gain_ref[:, columns]
        turned = cgrad_ref[:, columns] - shift_sum * cmask_ref[:, columns] - gain_sum * cnorm_ref[:, columns]
        total = cot_ext[16 : 16 + ROWS, columns].astype(F32) + scale * turned
        ginp_ref[:, columns] = jnp.where(live(ROWS, 0), total, 0.0).astype(BF16)

    write(ginp_ref, ginp_hbm, 1)

    @pl.loop(0, heads // 2)
    def _(pair):
        rows = pl.ds(pl.multiple_of(pair * 128, 128), 128)
        grad_context = dot(ginp_ref[...], w_ref[rows], ((1,), (1,))).astype(BF16).astype(F32)
        even, odd = pack_pair(grad_context)
        do_send[2 * pair] = even.astype(BF16)
        do_send[2 * pair + 1] = odd.astype(BF16)

    to_heads(do_send, do_recv, 13, 14)

    own_context = jnp.transpose(ctx_ref[HALO : HALO + ROWS].astype(F32)).astype(BF16)

    def stage0(piece):
        copy = remote(
            wsend.at[piece].at[other], g0.at[piece], piece_send.at[5 * piece + 0], piece_recv.at[5 * piece + 0], partner
        )
        copy.start()
        pending[f"stage 0 in {piece}"] = copy.wait_recv
        pending[f"stage 0 out {piece}"] = copy.wait_send

    for piece in range(PIECES):
        first = piece * piece_width
        size = min(piece_width, channels - first)
        if size > 0:
            terms = dot(own_context, ginp_ref[:, first : first + size]).astype(BF16)
            wsend.at[piece][:, :, :, :size] = terms.reshape(2, chips, 16, size)
        if piece < PIECES - 1:
            stage0(piece)

    tap_lanes = slice(piece_width - 128, piece_width)
    wsend[PIECES - 1, :, :, :, tap_lanes] = jnp.zeros((2, chips, 16, 128), BF16)

    @pl.loop(0, chunks)
    def _(chunk):
        columns = column(chunk)
        per_count = tot_ref[pl.ds(2 * chunks + chunk, 1)]
        gain_sum = sums_ref[pl.ds(chunk, 1)] * per_count
        shift_sum = sums_ref[pl.ds(chunks + chunk, 1)] * per_count
        scale = tot_ref[pl.ds(chunks + chunk, 1)] * gain_ref[:, columns]
        own = slice(16, 16 + ROWS)
        grad_conv = scale * (ga_ref[own, columns] - (shift_sum + conv_ref[own, columns] * gain_sum))
        grad_conv = jnp.where(live(ROWS, 0), grad_conv, 0.0)
        hidden = hid_ref[16:, columns]
        found = [None] * 32
        for low in range(8):
            moved = shifted(hidden, low)
            for high_part in range(4):
                tap = 8 * high_part + low - 1
                if 0 <= tap < KERNEL:
                    terms = grad_conv * moved[8 * high_part : 8 * high_part + ROWS]
                    found[tap] = jnp.sum(terms, axis=0, keepdims=True)
        found[31] = jnp.zeros((1, 128), F32)
        stacked = jnp.concatenate(found, axis=0).astype(BF16)
        wsend.at[PIECES - 1].at[0][pl.ds(chunk, 1), :, tap_lanes] = stacked[:16].reshape(1, 16, 128)
        wsend.at[PIECES - 1].at[1][pl.ds(chunk, 1), :, tap_lanes] = stacked[16:].reshape(1, 16, 128)

    stage0(PIECES - 1)

    def stage1(piece):
        settle(f"stage 0 in {piece}")

        @pl.loop(0, chips)
        def _(i):
            total = wsend.at[piece].at[core, i][...].astype(F32) + g0.at[piece].at[i][...].astype(F32)
            gs1.at[piece].at[i][...] = total.astype(BF16)

        g1.at[piece].at[chip][...] = gs1.at[piece].at[chip][...]

        @pl.loop(1, chips)
        def _(d):
            peer = (chip + d) % chips
            remote(
                gs1.at[piece].at[peer],
                g1.at[piece].at[chip],
                piece_send.at[5 * piece + 1],
                piece_recv.at[5 * piece + 1],
                (z, peer * 2 + core),
            ).start()

        later(f"stage 1 in {piece}", g1.at[piece].at[pl.ds(0, chips - 1)], piece_recv.at[5 * piece + 1])
        later(f"stage 1 out {piece}", g1.at[piece].at[pl.ds(0, chips - 1)], piece_send.at[5 * piece + 1])

    def stage2(piece):
        settle(f"stage 1 in {piece}")
        total = g1.at[piece][0].astype(F32)
        for i in range(1, chips):
            total = total + g1.at[piece][i].astype(F32)
        total = total.astype(BF16)
        gs2[piece] = total
        g2.at[piece].at[z][...] = total

        @pl.loop(1, depth)
        def _(d):
            remote(
                gs2.at[piece],
                g2.at[piece].at[z],
                piece_send.at[5 * piece + 2],
                piece_recv.at[5 * piece + 2],
                ((z + d) % depth, me),
            ).start()

        pending[f"stage 2 in {piece}"] = lambda: drain(
            g2.at[piece].at[pl.ds(0, depth - 1)], piece_recv.at[5 * piece + 2]
        )
        pending[f"stage 2 out {piece}"] = lambda: drain(
            g2.at[piece].at[pl.ds(0, depth - 1)], piece_send.at[5 * piece + 2]
        )

    def stage3(piece):
        settle(f"stage 2 in {piece}")
        total = g2.at[piece][0].astype(F32)
        for i in range(1, depth):
            total = total + g2.at[piece][i].astype(F32)
        gfin_ref.at[piece].at[core, chip][...] = total.astype(BF16)
        final = gfin_ref.at[piece].at[core, chip]

        @pl.loop(1, chips)
        def _(d):
            peer = (chip + d) % chips
            remote(
                final, final, piece_send.at[5 * piece + 3], piece_recv.at[5 * piece + 3], (z, peer * 2 + core)
            ).start()

        size = gfin_ref.at[piece].at[core, pl.ds(0, chips - 1)]
        later(f"stage 3 in {piece}", size, piece_recv.at[5 * piece + 3])
        later(f"stage 3 out {piece}", size, piece_send.at[5 * piece + 3])

    def stage4(piece):
        settle(f"stage 3 in {piece}")
        finals = gfin_ref.at[piece].at[core]
        copy = remote(finals, finals, piece_send.at[5 * piece + 4], piece_recv.at[5 * piece + 4], partner)
        copy.start()
        later(f"stage 4 in {piece}", gfin_ref.at[piece].at[other], piece_recv.at[5 * piece + 4])
        pending[f"stage 4 out {piece}"] = copy.wait_send

    for piece in range(PIECES):
        stage1(piece)

    settle("heads 13 in")
    for index in range(heads):
        rows = slice(ROWS * index, ROWS * index + ROWS)
        scaled = (unpack_high(do_recv[index].astype(F32)) * linv[rows]).astype(BF16)
        docl[rows] = scaled
        scaled = scaled.astype(F32)
        delta = jnp.sum(ctxh[rows] * scaled, axis=1, keepdims=True)
        first = delta.astype(BF16).astype(F32)
        rest = delta - first
        lane = lax.broadcasted_iota(jnp.int32, scaled.shape, 1)
        doaug[rows] = jnp.where(lane == 0, -first, jnp.where(lane == 1, -rest, scaled)).astype(BF16)

    dqt[...] = jnp.zeros_like(dqt)

    def part_copy(turn):
        rows = pl.ds(pl.multiple_of(turn * backward_block, backward_block), backward_block)
        return remote(dsend.at[rows], precv.at[rows], part_send.at[turn], part_recv.at[turn], partner)

    turns = 4
    slots = backward_block // ROWS

    @pl.loop(0, 2 * turns)
    def _(step):
        half = jnp.where(step < turns, other, core)
        turn = step % turns
        rows = pl.ds(
            pl.multiple_of(half * half_keys + turn * backward_block, backward_block), backward_block
        )
        turn_rows = pl.ds(pl.multiple_of(turn * backward_block, backward_block), backward_block)
        weights = pt[rows]
        grads = dot(v1[rows], doaug[...], ((1,), (1,))).astype(BF16)
        scores = weights * grads
        dqt[...] += dot(kt[:, rows], scores)
        rbuf[...] = dot(scores, qcl[...]) + dot(weights, docl[...])

        @pl.when(step < turns)
        def _():
            dsend[turn_rows] = rbuf[...].astype(BF16)
            part_copy(turn).start()

        @pl.when(step >= turns)
        def _():
            part_copy(turn).wait_recv()
            osend[turn_rows] = (rbuf[...] + precv[turn_rows].astype(F32)).astype(BF16)
            for i in range(slots):
                slot = turn * slots + i
                owner = (chip + chips - slot) % chips
                source = osend.at[pl.ds(pl.multiple_of(slot * ROWS, ROWS), ROWS)]

                def give(source=source, owner=owner):
                    remote(source, kvrecv.at[chip], own_sem, recv.at[20], (z, owner * 2 + core)).start()

                if i == 0:

                    @pl.when(turn == 0)
                    def _(source=source):
                        pltpu.make_async_copy(source, kvrecv.at[chip], recv.at[20]).start()

                    pl.when(turn > 0)(give)
                else:
                    give()

        for piece in range(PIECES):

            @pl.when(step == 3 + piece)
            def _(piece=piece):
                stage2(piece)

    def parts_sent():
        @pl.loop(0, turns)
        def _(turn):
            part_copy(turn).wait_send()

    pending["parts"] = parts_sent
    later("owned in", kvrecv, recv.at[20])
    later("owned out", kvrecv.at[pl.ds(0, chips - 1)], own_sem)

    @pl.loop(0, query_blocks)
    def _(block):
        part = pl.ds(pl.multiple_of(block * query_block, query_block), query_block)
        turned = dqt[:, part]
        turned = jnp.transpose(jnp.concatenate([turned, jnp.zeros_like(turned)], axis=0))
        half_part = pl.ds(pl.multiple_of(block * query_block // 2, query_block // 2), query_block // 2)
        dq_send[half_part] = pack_low(turned).astype(BF16)

    for i in range(heads):
        source = dq_send.at[pl.ds(64 * i, 64)]
        target = dq_recv.at[my_head]

        @pl.when(owner_of(i) == me)
        def _(source=source, target=target):
            pltpu.make_async_copy(source, target, recv.at[21]).start()

        @pl.when(owner_of(i) != me)
        def _(source=source, target=target, i=i):
            remote(source, target, dq_sem.at[i], recv.at[21], (z, owner_of(i))).start()

        def sent(source=source, i=i):
            @pl.when(owner_of(i) != me)
            def _():
                drain(source, dq_sem.at[i])

        pending[f"grad query {i}"] = sent

    for piece in range(PIECES):
        stage3(piece)

    settle("owned in")
    for pair in range(heads // 2):
        columns = slice(128 * pair, 128 * pair + 128)
        even = kvrecv[2 * pair].astype(F32) + kvrecv[2 * pair + heads].astype(F32)
        odd = kvrecv[2 * pair + 1].astype(F32) + kvrecv[2 * pair + 1 + heads].astype(F32)
        low = low_lanes(even.shape)
        gk_ref[:, columns] = jnp.where(low, even, roll64(odd)).astype(BF16)
        gv_ref[:, columns] = jnp.where(low, roll64(even), odd).astype(BF16)
    write(gk_ref, gk_hbm, 3)
    write(gv_ref, gv_hbm, 4)

    drain(dq_recv, recv.at[21])
    for pair in range(heads // 2):
        gq_ref[:, 128 * pair : 128 * pair + 128] = unpack_pair(
            dq_recv[2 * pair].astype(F32), dq_recv[2 * pair + 1].astype(F32)
        ).astype(BF16)

    write(gq_ref, gq_hbm, 2)
    for piece in range(PIECES):
        stage4(piece)
    settle()


def finish(width, chunks, *refs):
    out, ginp, gq, gk, gv, packed, sums = refs[:7]
    outs = refs[7:16]
    weights, taps, sem = refs[16:]
    channels = weights.shape[1]
    copies = [
        pltpu.make_async_copy(source, target, sem.at[index])
        for index, (source, target) in enumerate(
            (
                (out, outs[0]),
                (ginp, outs[1]),
                (gq, outs[2]),
                (gk, outs[3]),
                (gv, outs[4]),
                (weights, outs[5]),
                (taps, outs[6]),
                (sums.at[pl.ds(0, chunks)], outs[7]),
                (sums.at[pl.ds(chunks, chunks)], outs[8]),
            )
        )
    ]
    for index in (0, 1, 2, 3, 4, 7, 8):
        copies[index].start()
    piece_width = packed.shape[-1]
    for piece in range(PIECES):
        first = piece * piece_width
        size = min(piece_width, channels - first)
        for half in range(2 if size > 0 else 0):
            rows = slice(half * width // 2, (half + 1) * width // 2)
            terms = packed[piece, half, :, :, :size].astype(F32)
            weights[rows, first : first + size] = terms.reshape(width // 2, size)
    for chunk in range(chunks):
        lanes = slice(piece_width - 128, piece_width)
        columns = slice(128 * chunk, 128 * chunk + 128)
        taps[:16, columns] = packed[PIECES - 1, 0, chunk, :, lanes].astype(F32)
        taps[16:, columns] = packed[PIECES - 1, 1, chunk, :15, lanes].astype(F32)
    copies[5].start()
    copies[6].start()
    for copy in copies:
        copy.wait()


def shards(
    depth,
    query_rows,
    key_rows,
    value_rows,
    inputs,
    lengths,
    out_weight,
    taps,
    norm_gain,
    norm_shift,
    cotangent,
):
    seq = lax.axis_size("seq")
    heads = seq // 4
    chips = seq // 2
    width = query_rows.shape[2]
    channels = inputs.shape[2]
    chunks = channels // 128
    queries = ROWS * heads
    keys = seq * ROWS
    ext = ROWS + 2 * HALO
    mid = ROWS + 32
    padded = channels + 128
    piece_width = padded // PIECES
    query_block = min(queries, 512)
    vmem = pltpu.VMEM
    scratch = [
        vmem((ROWS, width), BF16),
        vmem((ROWS, width), BF16),
        vmem((ROWS, width), BF16),
        vmem((1, channels), F32),
        vmem((1, channels), F32),
        vmem((ROWS, channels), BF16),
        vmem((ROWS, channels), BF16),
        vmem((ROWS, width), BF16),
        vmem((ROWS, width), BF16),
        vmem((ROWS, width), BF16),
        vmem((8, 128), F32),
        vmem((depth, 8, 128), F32),
        vmem((ROWS, channels), F32),
        vmem((ROWS, channels), F32),
        vmem((ROWS, channels), F32),
        vmem((heads, ROWS, 128), BF16),
        vmem((heads, 64, 128), BF16),
        vmem((keys, 128), BF16),
        vmem((heads, 64, 128), BF16),
        vmem((keys, 128), BF16),
        vmem((keys, 128), BF16),
        vmem((64, keys), BF16),
        vmem((128, keys), BF16),
        vmem((queries, 128), BF16),
        vmem((queries, 128), BF16),
        vmem((2, keys, query_block), F32),
        vmem((keys, queries), BF16),
        vmem((queries, 128), F32),
        vmem((queries, 128), F32),
        vmem((queries // 2, 128), BF16),
        vmem((heads, ext // 2, 128), BF16),
        vmem((ext, channels), BF16),
        vmem((mid, channels), BF16),
        vmem((width, channels), BF16),
        vmem((KERNEL, channels), F32),
        vmem((ext, width), BF16),
        vmem((ext, channels), F32),
        vmem((mid, channels), F32),
        vmem((mid, channels), F32),
        vmem((2 * chunks, 128), F32),
        vmem((2 * chunks, 128), F32),
        vmem((2 * depth, 2 * chunks, 128), F32),
        vmem((chips, 2 * chunks, 128), F32),
        vmem((2 * chunks, 128), F32),
        vmem((2 * depth, 2 * chunks, 128), F32),
        vmem((2 * chunks, 128), F32),
        vmem((chips, 2 * chunks, 128), F32),
        vmem((3 * chunks, 128), F32),
        vmem((heads, 64, 128), BF16),
        vmem((heads, 64, 128), BF16),
        vmem((queries, 128), BF16),
        vmem((queries, 128), BF16),
        vmem((keys // 8, 128), F32),
        vmem((64, queries), F32),
        vmem((keys // 2, 128), BF16),
        vmem((keys // 2, 128), BF16),
        vmem((keys // 2, 128), BF16),
        vmem((chips, ROWS, 128), BF16),
        vmem((queries // 2, 128), BF16),
        vmem((heads, 64, 128), BF16),
        vmem((PIECES, 2, chips, 16, piece_width), BF16),
        vmem((PIECES, chips, 16, piece_width), BF16),
        vmem((PIECES, chips, 16, piece_width), BF16),
        vmem((PIECES, chips, 16, piece_width), BF16),
        vmem((PIECES, 16, piece_width), BF16),
        vmem((PIECES, depth, 16, piece_width), BF16),
        pltpu.SemaphoreType.DMA((9,)),
        pltpu.SemaphoreType.DMA((25,)),
        pltpu.SemaphoreType.DMA((25,)),
        pltpu.SemaphoreType.DMA((heads + 2,)),
        pltpu.SemaphoreType.DMA((heads,)),
        pltpu.SemaphoreType.DMA((4,)),
        pltpu.SemaphoreType.DMA((4,)),
        pltpu.SemaphoreType.DMA,
        pltpu.SemaphoreType.DMA((5 * PIECES,)),
        pltpu.SemaphoreType.DMA((5 * PIECES,)),
        pltpu.SemaphoreType.DMA((5,)),
    ]
    in_vmem = pl.BlockSpec(memory_space=pltpu.VMEM)
    anywhere = pl.BlockSpec(memory_space=pl.ANY)
    plain = (
        jax.ShapeDtypeStruct((ROWS, channels), BF16),
        jax.ShapeDtypeStruct((ROWS, channels), BF16),
        jax.ShapeDtypeStruct((ROWS, width), BF16),
        jax.ShapeDtypeStruct((ROWS, width), BF16),
        jax.ShapeDtypeStruct((ROWS, width), BF16),
    )
    results = pl.pallas_call(
        functools.partial(kernel, heads, seq, depth),
        out_shape=plain
        + (
            jax.ShapeDtypeStruct((PIECES, 2, chips, 16, piece_width), BF16),
            jax.ShapeDtypeStruct((2 * chunks, 128), F32),
        ),
        in_specs=[pl.BlockSpec(memory_space=pltpu.SMEM)] + [anywhere] * 9,
        out_specs=(anywhere,) * 5 + (in_vmem,) * 2,
        scratch_shapes=scratch,
        compiler_params=pltpu.CompilerParams(
            collective_id=0, has_side_effects=True, vmem_limit_bytes=60 * 1024 * 1024
        ),
    )(
        lengths,
        query_rows[0],
        key_rows[0],
        value_rows[0],
        inputs[0],
        cotangent[0],
        out_weight,
        taps,
        norm_gain[None],
        norm_shift[None],
    )
    final = pl.pallas_call(
        functools.partial(finish, width, chunks),
        out_shape=plain
        + (
            jax.ShapeDtypeStruct((width, channels), F32),
            jax.ShapeDtypeStruct((KERNEL, channels), F32),
            jax.ShapeDtypeStruct((chunks, 128), F32),
            jax.ShapeDtypeStruct((chunks, 128), F32),
        ),
        in_specs=[anywhere] * 5 + [in_vmem] * 2,
        out_specs=(anywhere,) * 9,
        scratch_shapes=[
            vmem((width, channels), F32),
            vmem((KERNEL, channels), F32),
            pltpu.SemaphoreType.DMA((9,)),
        ],
        compiler_params=pltpu.CompilerParams(vmem_limit_bytes=16 * 1024 * 1024),
    )(*results)
    return (
        *(array[None] for array in final[:5]),
        final[5],
        final[6],
        final[7].reshape(channels),
        final[8].reshape(channels),
    )


def solution(mesh):
    rows = P("dp", "seq", None)
    return jax.shard_map(
        functools.partial(shards, mesh.shape["dp"]),
        mesh=mesh,
        in_specs=(rows, rows, rows, rows, P("dp"), P(), P(), P(), P(), rows),
        out_specs=(rows, rows, rows, rows, rows, P(), P(), P(), P()),
        check_vma=False,
    )
```

time: 125 us -> 108 us (0.86)
  Pallas kernels: 114 us -> 99.7 us
  other arithmetic: 2.3 us -> 0 us
    pallas_call x1 -> x2, Pallas kernels: 114 us -> 99.7 us  [the longest x1 98 us: shards(): pl.pallas_call(functools.partial(kernel, heads, seq, depth), out_shape=pl...]
    unnamed x16 -> x14, local copies, waits for them, and re-layouts: 3.4 us -> 6.57 us
    convert_element_type x1 -> x0, other arithmetic: 1.63 us -> none  [shards(): packed[..., :channels].reshape(width, channels).astype(F32)]
    slice x1 -> x0, local copies, waits for them, and re-layouts: 1.3 us -> none  [shards(): packed[..., :channels].reshape(width, channels).astype(F32)]
    reshape x1 -> x0, local copies, waits for them, and re-layouts: 1.27 us -> none  [shards(): sums[chunks:].reshape(channels)]
where the time goes in v2:
time: 108 us
  Pallas kernels  99.7 us (92%)
  local copies, waits for them, and re-layouts  6.57 us (6%)
  between operations  1.31 us (1%)
    pallas_call x1, Pallas kernels, shards(): pl.pallas_call(functools.partial(kernel, heads, seq, depth), out_shape=pl...  98 us
    unnamed x14, local copies, waits for them, and re-layouts  6.57 us

profile of v2, /device:TPU:1, one launch (start us, length us, event | category | flops | bytes accessed | tf_op | source)
XLA Modules:
  0.0 107.6 jit_solution(5871294766334471989)
XLA Ops:
  1.3 98.0 %shard_map.169 = (bf16[128,1024]{1,0:T(8,128)(2,1)}, bf16[128,1024]{1,0:T(8,128)(2,1)}, bf16[128,512]{1,0:T(8,128)(2,1)}, bf16[128,512]{1,0:T(8,128)(2,1)}, bf16...) custom-call(s32[1]{0:T(128)S(6)} %copy.19.length_ref, bf16[128,512]{1,0:T(8,128)(2,1)} %bitcast.16, ...), custom_call_target="tpu_custom_call" | custom-call | tf_op jit(solution)/shard_map/pallas_call | solution.py:1079
  99.3 0.0 copy-start
  99.3 1.3 %copy-done = bf16[3,2,16,16,384]{4,3,2,1,0:T(8,128)(2,1)S(1)} copy-done((bf16[3,2,16,16,384]{4,3,2,1,0:T(8,128)(2,1)S(1)}, bf16[3,2,16,16,384]{4,3,2,1,0:T(8,128)(2,1)}, u32[]{:S(2)}) %copy-start) | copy-done | bytes 1179672
  100.6 0.0 copy-start.1
  100.6 0.9 copy-done.1
  101.5 0.0 copy-start.2
  101.5 0.9 copy-done.2
  102.5 0.0 copy-start.3
  102.5 0.9 copy-done.3
  103.4 0.0 copy-start.4
  103.4 0.9 copy-done.4
  104.3 0.0 copy-start.5
  104.3 0.9 copy-done.5
  105.2 0.0 copy-start.6
  105.2 0.7 copy-done.6
  105.9 1.7 %shard_map.170 = (bf16[128,1024]{1,0:T(8,128)(2,1)}, bf16[128,1024]{1,0:T(8,128)(2,1)}, bf16[128,512]{1,0:T(8,128)(2,1)}, bf16[128,512]{1,0:T(8,128)(2,1)}, bf16...) custom-call(bf16[128,1024]{1,0:T(8,128)(2,1)S(1)} %copy-done.1, ...), custom_call_target="tpu_custom_call" | custom-call | tf_op jit(solution)/shard_map/pallas_call | solution.py:1104
Async XLA Ops:
  99.3 1.3 %copy-start = (bf16[3,2,16,16,384]{4,3,2,1,0:T(8,128)(2,1)S(1)}, bf16[3,2,16,16,384]{4,3,2,1,0:T(8,128)(2,1)}, u32[]{:S(2)}) copy-start(bf16[3,2,16,16,384]{4,3,2,1,0:T(8,128)(2,1)} %get-tuple-element.30.refs_5_) | copy-start | bytes 3538948
  100.6 0.9 copy-start.1
  101.5 0.9 copy-start.2
  102.5 0.9 copy-start.3
  103.4 0.9 copy-start.4
  104.3 0.9 copy-start.5
  105.2 0.7 copy-start.6

commit v3 on v2

--- a/solution.py
+++ b/solution.py
@@ -118,6 +118,11 @@
     cmask_ref,
     cgrad_ref,
     cnorm_ref,
+    tmask_ref,
+    tgrad_ref,
+    tnorm_ref,
+    count_a,
+    count_b,
     kv_send,
     q_send,
     kvbuf,
@@ -231,10 +236,7 @@
 
     @pl.loop(1, depth)
     def _(d):
-        for c in range(2):
-            pl.semaphore_signal(
-                barrier, inc=1, device_id=((z + d) % depth, chip * 2 + c), device_id_type=MESH
-            )
+        pl.semaphore_signal(barrier, inc=1, device_id=((z + d) % depth, me), device_id_type=MESH)
 
     loads = (
         ("k", k_hbm, k_ref),
@@ -265,7 +267,7 @@
         q_send[2 * pair] = even.astype(BF16)
         q_send[2 * pair + 1] = odd.astype(BF16)
 
-    pl.semaphore_wait(barrier, seq - 1 + 2 * (depth - 1))
+    pl.semaphore_wait(barrier, seq - 1 + depth - 1)
 
     def kv_slot(d):
         return kvbuf.at[pl.ds(pl.multiple_of(core * half_keys + d * ROWS, ROWS), ROWS)]
@@ -492,6 +494,14 @@
         columns = column(chunk)
         cmask_ref[:, columns] = turned_convolution(jnp.where(live(mid, -16), 1.0, 0.0), columns)
 
+    settle("lengths in")
+    lengths = len_recv[:, :1]
+    count_a[...] = jnp.clip(lengths - (me * ROWS).astype(F32), 0.0, float(ROWS))
+    for i in range(seq):
+        count_b[i] = jnp.sum(jnp.clip(lengths - float(i * ROWS), 0.0, float(ROWS)), axis=0)
+    for target in (tmask_ref, tgrad_ref, tnorm_ref):
+        target[KERNEL:] = jnp.zeros((1, channels), F32)
+
     settle(*(f"halo {index} in" for index in range(4)))
     drain(ctx_recv, recv.at[8])
 
@@ -531,46 +541,52 @@
         stat_a[pl.ds(chunk, 1)] = summed
         stat_a[pl.ds(chunks + chunk, 1)] = squares
 
-    settle("lengths in")
-    lengths = len_recv[:, :1]
-
 
     def write(source, target, index):
         copy = pltpu.make_async_copy(source, target, write_sem.at[index])
         copy.start()
         pending[f"write {index}"] = copy.wait
 
-    def gather_first(source, target, index, beside=None):
-        slot = z * 2 + core
+    def gather(source, target, index, slot, count, peer, beside):
         target[slot] = source[...]
-        remote(source, target.at[slot], send.at[index], recv.at[index], partner).start()
-
-        @pl.loop(1, depth)
+
+        @pl.loop(1, count)
         def _(d):
-            for c in range(2):
-                remote(
-                    source, target.at[slot], send.at[index], recv.at[index], ((z + d) % depth, chip * 2 + c)
-                ).start()
-
-        later(f"first {index}", target.at[pl.ds(0, 2 * depth - 1)], send.at[index])
+            remote(source, target.at[slot], send.at[index], recv.at[index], peer(d)).start()
+
+        later(f"sums {index}", target.at[pl.ds(0, count - 1)], send.at[index])
         if beside is not None:
             beside()
-        drain(target.at[pl.ds(0, 2 * depth - 1)], recv.at[index])
-
-    def gather_second(source, target, index):
-        target[chip] = source[...]
-
-        @pl.loop(1, chips)
-        def _(d):
-            remote(
-                source, target.at[chip], send.at[index], recv.at[index], (z, ((chip + d) % chips) * 2 + core)
-            ).start()
-
-        later(f"second {index}", target.at[pl.ds(0, chips - 1)], send.at[index])
-        drain(target.at[pl.ds(0, chips - 1)], recv.at[index])
-
-    def frames_of(index):
-        return jnp.clip(lengths - (index * ROWS).astype(F32), 0.0, float(ROWS))
+        drain(target.at[pl.ds(0, count - 1)], recv.at[index])
+
+    def gather_first(source, target, index, beside=None):
+        gather(source, target, index, z, depth, lambda d: ((z + d) % depth, me), beside)
+
+    def gather_second(source, target, index, beside=None):
+        gather(source, target, index, me, seq, lambda d: (z, (me + d) % seq), beside)
+
+    def correlate(target, rows, columns):
+        hidden = hid_ref[16:, columns]
+        for low in range(8):
+            moved = shifted(hidden, low)
+            for high_part in range(4):
+                tap = 8 * high_part + low - 1
+                if 0 <= tap < KERNEL:
+                    terms = rows * moved[8 * high_part : 8 * high_part + ROWS]
+                    target[tap : tap + 1, columns] = jnp.sum(terms, axis=0, keepdims=True)
+
+    def correlate_mask():
+        @pl.loop(0, chunks)
+        def _(chunk):
+            correlate(tmask_ref, jnp.where(live(ROWS, 0), 1.0, 0.0), column(chunk))
+
+    def correlate_rest():
+        @pl.loop(0, chunks)
+        def _(chunk):
+            columns = column(chunk)
+            own = slice(16, 16 + ROWS)
+            correlate(tgrad_ref, ga_ref[own, columns], columns)
+            correlate(tnorm_ref, jnp.where(live(ROWS, 0), conv_ref[own, columns], 0.0), columns)
 
     def merged(gathered, counts):
         sums = gathered[:, :chunks]
@@ -581,23 +597,12 @@
         shift = sums / jnp.maximum(counts, 1.0) - mean[None]
         return total, jnp.sum(squares, axis=0) + jnp.sum(counts * shift * shift, axis=0), count, mean
 
-    def first_counts():
-        both_cores = [frames_of(chip * 2 + c) for c in range(2)]
-        return jnp.concatenate([lax.slice_in_dim(both_cores[i % 2], i // 2, i // 2 + 1) for i in range(2 * depth)], axis=0)
-
-    def second_counts():
-        per_chip = []
-        for i in range(chips):
-            first = jnp.clip(lengths - float(2 * i * ROWS), 0.0, float(2 * ROWS))
-            per_chip.append(jnp.sum(first, axis=0, keepdims=True))
-        return jnp.concatenate(per_chip, axis=0)
-
-    gather_first(stat_a, recv_a, 9)
-    total, squares, count, mean = merged(recv_a[...], first_counts())
+    gather_first(stat_a, recv_a, 9, correlate_mask)
+    total, squares, count, mean = merged(recv_a[...], count_a[...])
     stat_b[:chunks] = total
     stat_b[chunks:] = squares
     gather_second(stat_b, recv_b, 10)
-    total, squares, count, mean = merged(recv_b[...], second_counts())
+    total, squares, count, mean = merged(recv_b[...], count_b[...])
     tot_ref[:chunks] = mean
     tot_ref[chunks : 2 * chunks] = lax.rsqrt(squares / count + EPSILON)
     tot_ref[2 * chunks : 3 * chunks] = jnp.broadcast_to(1.0 / count, (chunks, 128))
@@ -634,7 +639,7 @@
 
     gather_first(stat_c, recv_c, 11, beside)
     stat_d[...] = jnp.sum(recv_c[...], axis=0)
-    gather_second(stat_d, recv_d, 12)
+    gather_second(stat_d, recv_d, 12, correlate_rest)
     sums_ref[...] = jnp.sum(recv_d[...], axis=0)
 
     @pl.loop(0, chunks)
@@ -690,20 +695,8 @@
         gain_sum = sums_ref[pl.ds(chunk, 1)] * per_count
         shift_sum = sums_ref[pl.ds(chunks + chunk, 1)] * per_count
         scale = tot_ref[pl.ds(chunks + chunk, 1)] * gain_ref[:, columns]
-        own = slice(16, 16 + ROWS)
-        grad_conv = scale * (ga_ref[own, columns] - (shift_sum + conv_ref[own, columns] * gain_sum))
-        grad_conv = jnp.where(live(ROWS, 0), grad_conv, 0.0)
-        hidden = hid_ref[16:, columns]
-        found = [None] * 32
-        for low in range(8):
-            moved = shifted(hidden, low)
-            for high_part in range(4):
-                tap = 8 * high_part + low - 1
-                if 0 <= tap < KERNEL:
-                    terms = grad_conv * moved[8 * high_part : 8 * high_part + ROWS]
-                    found[tap] = jnp.sum(terms, axis=0, keepdims=True)
-        found[31] = jnp.zeros((1, 128), F32)
-        stacked = jnp.concatenate(found, axis=0).astype(BF16)
+        stacked = tgrad_ref[:, columns] - shift_sum * tmask_ref[:, columns] - gain_sum * tnorm_ref[:, columns]
+        stacked = (scale * stacked).astype(BF16)
         wsend.at[PIECES - 1].at[0][pl.ds(chunk, 1), :, tap_lanes] = stacked[:16].reshape(1, 16, 128)
         wsend.at[PIECES - 1].at[1][pl.ds(chunk, 1), :, tap_lanes] = stacked[16:].reshape(1, 16, 128)
 
@@ -712,11 +705,8 @@
     def stage1(piece):
         settle(f"stage 0 in {piece}")
 
-        @pl.loop(0, chips)
-        def _(i):
-            total = wsend.at[piece].at[core, i][...].astype(F32) + g0.at[piece].at[i][...].astype(F32)
-            gs1.at[piece].at[i][...] = total.astype(BF16)
-
+        total = wsend.at[piece].at[core][...].astype(F32) + g0[piece].astype(F32)
+        gs1[piece] = total.astype(BF16)
         g1.at[piece].at[chip][...] = gs1.at[piece].at[chip][...]
 
         @pl.loop(1, chips)
@@ -853,7 +843,7 @@
 
         for piece in range(PIECES):
 
-            @pl.when(step == 3 + piece)
+            @pl.when(step == 2 + piece)
             def _(piece=piece):
                 stage2(piece)
 
@@ -1004,6 +994,11 @@
         vmem((ROWS, channels), F32),
         vmem((ROWS, channels), F32),
         vmem((ROWS, channels), F32),
+        vmem((KERNEL + 1, channels), F32),
+        vmem((KERNEL + 1, channels), F32),
+        vmem((KERNEL + 1, channels), F32),
+        vmem((depth, 1, 128), F32),
+        vmem((seq, 1, 128), F32),
         vmem((heads, ROWS, 128), BF16),
         vmem((heads, 64, 128), BF16),
         vmem((keys, 128), BF16),
@@ -1030,12 +1025,12 @@
         vmem((mid, channels), F32),
         vmem((2 * chunks, 128), F32),
         vmem((2 * chunks, 128), F32),
-        vmem((2 * depth, 2 * chunks, 128), F32),
-        vmem((chips, 2 * chunks, 128), F32),
+        vmem((depth, 2 * chunks, 128), F32),
+        vmem((seq, 2 * chunks, 128), F32),
         vmem((2 * chunks, 128), F32),
-        vmem((2 * depth, 2 * chunks, 128), F32),
+        vmem((depth, 2 * chunks, 128), F32),
         vmem((2 * chunks, 128), F32),
-        vmem((chips, 2 * chunks, 128), F32),
+        vmem((seq, 2 * chunks, 128), F32),
         vmem((3 * chunks, 128), F32),
         vmem((heads, 64, 128), BF16),
         vmem((heads, 64, 128), BF16),
@@ -1117,7 +1112,7 @@
             vmem((KERNEL, channels), F32),
             pltpu.SemaphoreType.DMA((9,)),
         ],
-        compiler_params=pltpu.CompilerParams(vmem_limit_bytes=16 * 1024 * 1024),
+        compiler_params=pltpu.CompilerParams(vmem_limit_bytes=60 * 1024 * 1024),
     )(*results)
     return (
         *(array[None] for array in final[:5]),

time: 108 us -> 129 us (1.19)
  Pallas kernels: 99.7 us -> 127 us
  local copies, waits for them, and re-layouts: 6.57 us -> 0 us
    pallas_call x1, Pallas kernels: 1.73 us -> 30.3 us  [shards(): pl.pallas_call(functools.partial(finish, width, chunks), out_shape=plain...]
    unnamed x14 -> x0, local copies, waits for them, and re-layouts: 6.57 us -> none
where the time goes in v3:
time: 129 us
  Pallas kernels  127 us (98%)
  between operations  1.3 us (1%)
    pallas_call x1, Pallas kernels, shards(): pl.pallas_call(functools.partial(kernel, heads, seq, depth), out_shape=pl...  97.1 us
    pallas_call x1, Pallas kernels, shards(): pl.pallas_call(functools.partial(finish, width, chunks), out_shape=plain...  30.3 us

profile of v3, /device:TPU:1, one launch (start us, length us, event | category | flops | bytes accessed | tf_op | source)
XLA Modules:
  0.0 128.7 jit_solution(8625643585525333041)
XLA Ops:
  1.3 97.1 %shard_map.169 = (bf16[128,1024]{1,0:T(8,128)(2,1)}, bf16[128,1024]{1,0:T(8,128)(2,1)}, bf16[128,512]{1,0:T(8,128)(2,1)}, bf16[128,512]{1,0:T(8,128)(2,1)}, bf16...) custom-call(s32[1]{0:T(128)S(6)} %copy.19.length_ref, bf16[128,512]{1,0:T(8,128)(2,1)} %bitcast.16, ...), custom_call_target="tpu_custom_call" | custom-call | tf_op jit(solution)/shard_map/pallas_call | solution.py:1074
  98.4 30.3 %shard_map.170 = (bf16[128,1024]{1,0:T(8,128)(2,1)}, bf16[128,1024]{1,0:T(8,128)(2,1)}, bf16[128,512]{1,0:T(8,128)(2,1)}, bf16[128,512]{1,0:T(8,128)(2,1)}, bf16...) custom-call(bf16[128,1024]{1,0:T(8,128)(2,1)} %get-tuple-element.25., ...), custom_call_target="tpu_custom_call" | custom-call | tf_op jit(solution)/shard_map/pallas_call | solution.py:1099

commit v4 on v3

--- a/solution.py
+++ b/solution.py
@@ -910,10 +910,17 @@
 
 
 def finish(width, chunks, *refs):
-    out, ginp, gq, gk, gv, packed, sums = refs[:7]
+    sources = refs[:7]
     outs = refs[7:16]
-    weights, taps, sem = refs[16:]
+    out, ginp, gq, gk, gv, packed, sums = refs[16:23]
+    weights, taps, load_sem, sem = refs[23:]
     channels = weights.shape[1]
+    loads = [
+        pltpu.make_async_copy(source, target, load_sem.at[index])
+        for index, (source, target) in enumerate(zip(sources, refs[16:23]))
+    ]
+    for index in (5, 6, 0, 1, 2, 3, 4):
+        loads[index].start()
     copies = [
         pltpu.make_async_copy(source, target, sem.at[index])
         for index, (source, target) in enumerate(
@@ -930,8 +937,7 @@
             )
         )
     ]
-    for index in (0, 1, 2, 3, 4, 7, 8):
-        copies[index].start()
+    loads[5].wait()
     piece_width = packed.shape[-1]
     for piece in range(PIECES):
         first = piece * piece_width
@@ -947,6 +953,12 @@
         taps[16:, columns] = packed[PIECES - 1, 1, chunk, :15, lanes].astype(F32)
     copies[5].start()
     copies[6].start()
+    loads[6].wait()
+    copies[7].start()
+    copies[8].start()
+    for index in range(5):
+        loads[index].wait()
+        copies[index].start()
     for copy in copies:
         copy.wait()
 
@@ -1105,11 +1117,13 @@
             jax.ShapeDtypeStruct((chunks, 128), F32),
             jax.ShapeDtypeStruct((chunks, 128), F32),
         ),
-        in_specs=[anywhere] * 5 + [in_vmem] * 2,
+        in_specs=[anywhere] * 7,
         out_specs=(anywhere,) * 9,
-        scratch_shapes=[
+        scratch_shapes=[vmem(array.shape, array.dtype) for array in results]
+        + [
             vmem((width, channels), F32),
             vmem((KERNEL, channels), F32),
+            pltpu.SemaphoreType.DMA((7,)),
             pltpu.SemaphoreType.DMA((9,)),
         ],
         compiler_params=pltpu.CompilerParams(vmem_limit_bytes=60 * 1024 * 1024),

time: 129 us -> 102 us (0.79)
  Pallas kernels: 127 us -> 100 us
    pallas_call x1, Pallas kernels: 30.3 us -> 3.21 us  [shards(): pl.pallas_call(functools.partial(finish, width, chunks), out_shape=plain...]
where the time goes in v4:
time: 102 us
  Pallas kernels  100 us (98%)
  between operations  1.3 us (1%)
    pallas_call x1, Pallas kernels, shards(): pl.pallas_call(functools.partial(kernel, heads, seq, depth), out_shape=pl...  97.1 us
    pallas_call x1, Pallas kernels, shards(): pl.pallas_call(functools.partial(finish, width, chunks), out_shape=plain...  3.21 us

profile of v4, /device:TPU:1, one launch (start us, length us, event | category | flops | bytes accessed | tf_op | source)
XLA Modules:
  0.0 101.6 jit_solution(6725467649857004321)
XLA Ops:
  1.3 97.1 %shard_map.169 = (bf16[128,1024]{1,0:T(8,128)(2,1)}, bf16[128,1024]{1,0:T(8,128)(2,1)}, bf16[128,512]{1,0:T(8,128)(2,1)}, bf16[128,512]{1,0:T(8,128)(2,1)}, bf16...) custom-call(s32[1]{0:T(128)S(6)} %copy.19.length_ref, bf16[128,512]{1,0:T(8,128)(2,1)} %bitcast.16, ...), custom_call_target="tpu_custom_call" | custom-call | tf_op jit(solution)/shard_map/pallas_call | solution.py:1086
  98.4 3.2 %shard_map.170 = (bf16[128,1024]{1,0:T(8,128)(2,1)}, bf16[128,1024]{1,0:T(8,128)(2,1)}, bf16[128,512]{1,0:T(8,128)(2,1)}, bf16[128,512]{1,0:T(8,128)(2,1)}, bf16...) custom-call(bf16[128,1024]{1,0:T(8,128)(2,1)} %get-tuple-element.25., ...), custom_call_target="tpu_custom_call" | custom-call | tf_op jit(solution)/shard_map/pallas_call | solution.py:1111

commit v5 on v4

--- a/solution.py
+++ b/solution.py
@@ -118,6 +118,7 @@
     cmask_ref,
     cgrad_ref,
     cnorm_ref,
+    own_ctx,
     tmask_ref,
     tgrad_ref,
     tnorm_ref,
@@ -228,15 +229,22 @@
         for name in names or tuple(pending):
             pending.pop(name)()
 
+    def around(count, act):
+        act(count // 2)
+
+        @pl.loop(1, count // 2)
+        def _(k):
+            act(count // 2 + k)
+            act(count // 2 - k)
+
     barrier = pltpu.get_barrier_semaphore()
 
-    @pl.loop(1, seq)
-    def _(d):
-        pl.semaphore_signal(barrier, inc=1, device_id=(z, (me + d) % seq), device_id_type=MESH)
-
-    @pl.loop(1, depth)
-    def _(d):
-        pl.semaphore_signal(barrier, inc=1, device_id=((z + d) % depth, me), device_id_type=MESH)
+    def greet(device):
+        pl.semaphore_signal(barrier, inc=1, device_id=device, device_id_type=MESH)
+
+    around(depth, lambda d: greet(((z + d) % depth, me)))
+    around(seq, lambda d: greet((z, (me + d) % seq)))
+
 
     loads = (
         ("k", k_hbm, k_ref),
@@ -550,9 +558,10 @@
     def gather(source, target, index, slot, count, peer, beside):
         target[slot] = source[...]
 
-        @pl.loop(1, count)
-        def _(d):
-            remote(source, target.at[slot], send.at[index], recv.at[index], peer(d)).start()
+        around(
+            count,
+            lambda d: remote(source, target.at[slot], send.at[index], recv.at[index], peer(d)).start(),
+        )
 
         later(f"sums {index}", target.at[pl.ds(0, count - 1)], send.at[index])
         if beside is not None:
@@ -576,6 +585,8 @@
                     target[tap : tap + 1, columns] = jnp.sum(terms, axis=0, keepdims=True)
 
     def correlate_mask():
+        own_ctx[...] = jnp.transpose(ctx_ref[HALO : HALO + ROWS].astype(F32)).astype(BF16)
+
         @pl.loop(0, chunks)
         def _(chunk):
             correlate(tmask_ref, jnp.where(live(ROWS, 0), 1.0, 0.0), column(chunk))
@@ -656,18 +667,6 @@
 
     write(ginp_ref, ginp_hbm, 1)
 
-    @pl.loop(0, heads // 2)
-    def _(pair):
-        rows = pl.ds(pl.multiple_of(pair * 128, 128), 128)
-        grad_context = dot(ginp_ref[...], w_ref[rows], ((1,), (1,))).astype(BF16).astype(F32)
-        even, odd = pack_pair(grad_context)
-        do_send[2 * pair] = even.astype(BF16)
-        do_send[2 * pair + 1] = odd.astype(BF16)
-
-    to_heads(do_send, do_recv, 13, 14)
-
-    own_context = jnp.transpose(ctx_ref[HALO : HALO + ROWS].astype(F32)).astype(BF16)
-
     def stage0(piece):
         copy = remote(
             wsend.at[piece].at[other], g0.at[piece], piece_send.at[5 * piece + 0], piece_recv.at[5 * piece + 0], partner
@@ -680,7 +679,7 @@
         first = piece * piece_width
         size = min(piece_width, channels - first)
         if size > 0:
-            terms = dot(own_context, ginp_ref[:, first : first + size]).astype(BF16)
+            terms = dot(own_ctx[...], ginp_ref[:, first : first + size]).astype(BF16)
             wsend.at[piece][:, :, :, :size] = terms.reshape(2, chips, 16, size)
         if piece < PIECES - 1:
             stage0(piece)
@@ -701,6 +700,16 @@
         wsend.at[PIECES - 1].at[1][pl.ds(chunk, 1), :, tap_lanes] = stacked[16:].reshape(1, 16, 128)
 
     stage0(PIECES - 1)
+
+    @pl.loop(0, heads // 2)
+    def _(pair):
+        rows = pl.ds(pl.multiple_of(pair * 128, 128), 128)
+        grad_context = dot(ginp_ref[...], w_ref[rows], ((1,), (1,))).astype(BF16).astype(F32)
+        even, odd = pack_pair(grad_context)
+        do_send[2 * pair] = even.astype(BF16)
+        do_send[2 * pair + 1] = odd.astype(BF16)
+
+    to_heads(do_send, do_recv, 13, 14)
 
     def stage1(piece):
         settle(f"stage 0 in {piece}")
@@ -1006,6 +1015,7 @@
         vmem((ROWS, channels), F32),
         vmem((ROWS, channels), F32),
         vmem((ROWS, channels), F32),
+        vmem((width, ROWS), BF16),
         vmem((KERNEL + 1, channels), F32),
         vmem((KERNEL + 1, channels), F32),
         vmem((KERNEL + 1, channels), F32),

time: 102 us -> 101 us (level)
  no operation moved by 1% of the time
where the time goes in v5:
time: 101 us
  Pallas kernels  100 us (99%)
  between operations  1.3 us (1%)
    pallas_call x1, Pallas kernels, shards(): pl.pallas_call(functools.partial(kernel, heads, seq, depth), out_shape=pl...  96.8 us
    pallas_call x1, Pallas kernels, shards(): pl.pallas_call(functools.partial(finish, width, chunks), out_shape=plain...  3.21 us

profile of v5, /device:TPU:1, one launch (start us, length us, event | category | flops | bytes accessed | tf_op | source)
XLA Modules:
  0.0 101.3 jit_solution(494692954409021372)
XLA Ops:
  1.3 96.8 %shard_map.169 = (bf16[128,1024]{1,0:T(8,128)(2,1)}, bf16[128,1024]{1,0:T(8,128)(2,1)}, bf16[128,512]{1,0:T(8,128)(2,1)}, bf16[128,512]{1,0:T(8,128)(2,1)}, bf16...) custom-call(s32[1]{0:T(128)S(6)} %copy.19.length_ref, bf16[128,512]{1,0:T(8,128)(2,1)} %bitcast.16, ...), custom_call_target="tpu_custom_call" | custom-call | tf_op jit(solution)/shard_map/pallas_call | solution.py:1096
  98.1 3.2 %shard_map.170 = (bf16[128,1024]{1,0:T(8,128)(2,1)}, bf16[128,1024]{1,0:T(8,128)(2,1)}, bf16[128,512]{1,0:T(8,128)(2,1)}, bf16[128,512]{1,0:T(8,128)(2,1)}, bf16...) custom-call(bf16[128,1024]{1,0:T(8,128)(2,1)} %get-tuple-element.25., ...), custom_call_target="tpu_custom_call" | custom-call | tf_op jit(solution)/shard_map/pallas_call | solution.py:1121

commit v6 on v5

--- a/solution.py
+++ b/solution.py
@@ -701,16 +701,6 @@
 
     stage0(PIECES - 1)
 
-    @pl.loop(0, heads // 2)
-    def _(pair):
-        rows = pl.ds(pl.multiple_of(pair * 128, 128), 128)
-        grad_context = dot(ginp_ref[...], w_ref[rows], ((1,), (1,))).astype(BF16).astype(F32)
-        even, odd = pack_pair(grad_context)
-        do_send[2 * pair] = even.astype(BF16)
-        do_send[2 * pair + 1] = odd.astype(BF16)
-
-    to_heads(do_send, do_recv, 13, 14)
-
     def stage1(piece):
         settle(f"stage 0 in {piece}")
 
@@ -732,6 +722,19 @@
         later(f"stage 1 in {piece}", g1.at[piece].at[pl.ds(0, chips - 1)], piece_recv.at[5 * piece + 1])
         later(f"stage 1 out {piece}", g1.at[piece].at[pl.ds(0, chips - 1)], piece_send.at[5 * piece + 1])
 
+    for piece in range(PIECES - 1):
+        stage1(piece)
+
+    @pl.loop(0, heads // 2)
+    def _(pair):
+        rows = pl.ds(pl.multiple_of(pair * 128, 128), 128)
+        grad_context = dot(ginp_ref[...], w_ref[rows], ((1,), (1,))).astype(BF16).astype(F32)
+        even, odd = pack_pair(grad_context)
+        do_send[2 * pair] = even.astype(BF16)
+        do_send[2 * pair + 1] = odd.astype(BF16)
+
+    to_heads(do_send, do_recv, 13, 14)
+
     def stage2(piece):
         settle(f"stage 1 in {piece}")
         total = g1.at[piece][0].astype(F32)
@@ -773,9 +776,12 @@
                 final, final, piece_send.at[5 * piece + 3], piece_recv.at[5 * piece + 3], (z, peer * 2 + core)
             ).start()
 
-        size = gfin_ref.at[piece].at[core, pl.ds(0, chips - 1)]
-        later(f"stage 3 in {piece}", size, piece_recv.at[5 * piece + 3])
-        later(f"stage 3 out {piece}", size, piece_send.at[5 * piece + 3])
+        pending[f"stage 3 in {piece}"] = lambda: drain(
+            gfin_ref.at[piece].at[core, pl.ds(0, chips - 1)], piece_recv.at[5 * piece + 3]
+        )
+        pending[f"stage 3 out {piece}"] = lambda: drain(
+            gfin_ref.at[piece].at[core, pl.ds(0, chips - 1)], piece_send.at[5 * piece + 3]
+        )
 
     def stage4(piece):
         settle(f"stage 3 in {piece}")
@@ -785,8 +791,7 @@
         later(f"stage 4 in {piece}", gfin_ref.at[piece].at[other], piece_recv.at[5 * piece + 4])
         pending[f"stage 4 out {piece}"] = copy.wait_send
 
-    for piece in range(PIECES):
-        stage1(piece)
+    stage1(PIECES - 1)
 
     settle("heads 13 in")
     for index in range(heads):
@@ -856,6 +861,14 @@
             def _(piece=piece):
                 stage2(piece)
 
+        for piece in range(PIECES - 1):
+
+            @pl.when(step == 6 + piece)
+            def _(piece=piece):
+                stage3(piece)
+
+    stage3(PIECES - 1)
+
     def parts_sent():
         @pl.loop(0, turns)
         def _(turn):
@@ -891,9 +904,6 @@
                 drain(source, dq_sem.at[i])
 
         pending[f"grad query {i}"] = sent
-
-    for piece in range(PIECES):
-        stage3(piece)
 
     settle("owned in")
     for pair in range(heads // 2):

time: 101 us -> 105 us (1.040)
  Pallas kernels: 100 us -> 104 us
    pallas_call x1, Pallas kernels: 96.8 us -> 100 us  [shards(): pl.pallas_call(functools.partial(kernel, heads, seq, depth), out_shape=pl...]
where the time goes in v6:
time: 105 us
  Pallas kernels  104 us (99%)
  between operations  1.3 us (1%)
    pallas_call x1, Pallas kernels, shards(): pl.pallas_call(functools.partial(kernel, heads, seq, depth), out_shape=pl...  100 us
    pallas_call x1, Pallas kernels, shards(): pl.pallas_call(functools.partial(finish, width, chunks), out_shape=plain...  3.21 us

profile of v6, /device:TPU:1, one launch (start us, length us, event | category | flops | bytes accessed | tf_op | source)
XLA Modules:
  0.0 104.9 jit_solution(9101152082802443443)
XLA Ops:
  1.3 100.4 %shard_map.169 = (bf16[128,1024]{1,0:T(8,128)(2,1)}, bf16[128,1024]{1,0:T(8,128)(2,1)}, bf16[128,512]{1,0:T(8,128)(2,1)}, bf16[128,512]{1,0:T(8,128)(2,1)}, bf16...) custom-call(s32[1]{0:T(128)S(6)} %copy.19.length_ref, bf16[128,512]{1,0:T(8,128)(2,1)} %bitcast.16, ...), custom_call_target="tpu_custom_call" | custom-call | tf_op jit(solution)/shard_map/pallas_call | solution.py:1106
  101.7 3.2 %shard_map.170 = (bf16[128,1024]{1,0:T(8,128)(2,1)}, bf16[128,1024]{1,0:T(8,128)(2,1)}, bf16[128,512]{1,0:T(8,128)(2,1)}, bf16[128,512]{1,0:T(8,128)(2,1)}, bf16...) custom-call(bf16[128,1024]{1,0:T(8,128)(2,1)} %get-tuple-element.25., ...), custom_call_target="tpu_custom_call" | custom-call | tf_op jit(solution)/shard_map/pallas_call | solution.py:1131

commit v7 on v5

--- a/solution.py
+++ b/solution.py
@@ -852,7 +852,7 @@
 
         for piece in range(PIECES):
 
-            @pl.when(step == 2 + piece)
+            @pl.when(step == 3 + piece)
             def _(piece=piece):
                 stage2(piece)
 

time: 101 us -> 101 us (level)
  no operation moved by 1% of the time
where the time goes in v7:
time: 101 us
  Pallas kernels  100 us (99%)
  between operations  1.3 us (1%)
    pallas_call x1, Pallas kernels, shards(): pl.pallas_call(functools.partial(kernel, heads, seq, depth), out_shape=pl...  96.8 us
    pallas_call x1, Pallas kernels, shards(): pl.pallas_call(functools.partial(finish, width, chunks), out_shape=plain...  3.21 us

profile of v7, /device:TPU:1, one launch (start us, length us, event | category | flops | bytes accessed | tf_op | source)
XLA Modules:
  0.0 101.3 jit_solution(17438002488088076461)
XLA Ops:
  1.3 96.8 %shard_map.169 = (bf16[128,1024]{1,0:T(8,128)(2,1)}, bf16[128,1024]{1,0:T(8,128)(2,1)}, bf16[128,512]{1,0:T(8,128)(2,1)}, bf16[128,512]{1,0:T(8,128)(2,1)}, bf16...) custom-call(s32[1]{0:T(128)S(6)} %copy.19.length_ref, bf16[128,512]{1,0:T(8,128)(2,1)} %bitcast.16, ...), custom_call_target="tpu_custom_call" | custom-call | tf_op jit(solution)/shard_map/pallas_call | solution.py:1096
  98.1 3.2 %shard_map.170 = (bf16[128,1024]{1,0:T(8,128)(2,1)}, bf16[128,1024]{1,0:T(8,128)(2,1)}, bf16[128,512]{1,0:T(8,128)(2,1)}, bf16[128,512]{1,0:T(8,128)(2,1)}, bf16...) custom-call(bf16[128,1024]{1,0:T(8,128)(2,1)} %get-tuple-element.25., ...), custom_call_target="tpu_custom_call" | custom-call | tf_op jit(solution)/shard_map/pallas_call | solution.py:1121
